TPU v7x, 512 devices: a whole 4x4x16 slice. The times are simulated.
512 devices in a mesh: blk: 64 (over x_lo, z, core), group: 8 (over y, x_hi).
Axes of the slice: x: 4 (x_hi: 2, x_lo: 2; x = x_hi * 2 + x_lo), y: 4, z: 16, core: 2. Of those that a mesh axis runs over, the one named last changes fastest.
Arguments:
- queries: bfloat16 [65536, 768], P(('blk', 'group')), may hold values from -6 to 6
- keys: bfloat16 [16384, 768], P(('blk', 'group')), may hold values from -6 to 6
- labels: bfloat16 [16384, 512], P(('blk', 'group')), may hold values from -6 to 6
Outputs:
- soft_labels: bfloat16 [65536, 512], P(('blk', 'group'))
All inputs are finite; a program needn't handle non-finite values.
Results may differ from a plain program's by a relative error of at most 0.0035.
Values may be sent and summed in bfloat16 or wider, within the bound.
No kernel may reach another device: no remote copies, remote signals or barrier semaphores. Data moves between devices by JAX's collectives and lax.ppermute only.
A program may use at most 64 MiB of HBM per device.

v0:
```python
import math

import jax
import jax.numpy as jnp
from jax import lax
from jax.sharding import PartitionSpec as P


def shifted(value, axis, by):
    devices = lax.axis_size(axis)
    return lax.ppermute(value, axis, [(i, (i + by) % devices) for i in range(devices)])


def update(partial_value, visiting, row_keys, label_values, sharpness):
    row_max, row_sum, weighted = partial_value
    scores = (
        lax.dot_general(
            visiting, row_keys, (((1,), (1,)), ((), ())), preferred_element_type=jnp.float32
        )
        * sharpness
    )
    new_max = jnp.maximum(row_max, jnp.max(scores, axis=1))
    rescale = jnp.exp(row_max - new_max)
    weights = jnp.exp(scores - new_max[:, None])
    row_sum = row_sum * rescale + jnp.sum(weights, axis=1)
    weighted = weighted * rescale[:, None] + jnp.dot(
        weights, label_values, preferred_element_type=jnp.float32, precision=lax.Precision.HIGHEST
    )
    return (new_max, row_sum, weighted)


def starting(count, classes):
    return (
        jnp.full((count,), -jnp.inf, jnp.float32),
        jnp.zeros((count,), jnp.float32),
        jnp.zeros((count, classes), jnp.float32),
    )


def shards(queries, keys, labels):
    features = queries.shape[1]
    classes = labels.shape[1]
    count = queries.shape[0]
    sharpness = 2.5 / math.sqrt(features)
    groups = lax.axis_size("group")
    all_keys, all_labels = (
        lax.all_gather(keys, "blk", axis=0, tiled=True),
        lax.all_gather(labels, "blk", axis=0, tiled=True),
    )
    label_values = all_labels.astype(jnp.float32)
    partial_value = starting(count, classes)
    visiting = queries
    for hop_index in range(groups):
        partial_value = update(partial_value, visiting, all_keys, label_values, sharpness)
        if hop_index < groups - 1:
            visiting, row_max, row_sum, weighted = (
                shifted(visiting.astype(jnp.float32), "group", 1).astype(visiting.dtype),
                shifted(partial_value[0], "group", 1),
                shifted(partial_value[1], "group", 1),
                shifted(partial_value[2], "group", 1),
            )
            partial_value = (row_max, row_sum, weighted)
        else:
            partial_value = shifted(
                (partial_value[0], partial_value[1], partial_value[2]), "group", 1
            )
    row_max, row_sum, weighted = partial_value
    return (weighted / row_sum[:, None]).astype(jnp.bfloat16)


def solution(mesh):
    placed = (P(("blk", "group"), None), P(("blk", "group"), None), P(("blk", "group"), None))
    return jax.shard_map(
        shards, mesh=mesh, in_specs=placed, out_specs=P(("blk", "group"), None), check_vma=False
    )
```

profile of v0, /device:TPU:32, one launch (start us, length us, event | category | flops | bytes accessed | tf_op | source)
XLA Modules:
  0.0 393.3 jit_solution(14396318715785657147)
XLA Ops:
  8.0 4.9 %collective-permute-start.2 = (bf16[128,768]{1,0:T(8,128)(2,1)}, bf16[128,768]{1,0:T(8,128)(2,1)S(1)}, u32[]{:S(2)}, u32[]{:S(2)}) collective-permute-start(bf16[128,768]{1,0:T(8,128)(2,1)} %param.3), channel_id=1, source_target_pairs={{0,1},{1,2},{2,3},{3,4},{4,5},{5,6},{6,7},{7,0},{8,9},{9,10},{10,1... | collective-permute-start | bytes 589832 | tf_op jit(solution)/shard_map/ppermute | solution.py:11
  12.9 7.5 %collective-permute-done.2 = bf16[128,768]{1,0:T(8,128)(2,1)S(1)} collective-permute-done((bf16[128,768]{1,0:T(8,128)(2,1)}, bf16[128,768]{1,0:T(8,128)(2,1)S(1)}, u32[]{:S(2)}, u32[]{:S(2)}) %collective-permute-start.2) | collective-permute-done | bytes 196640 | tf_op jit(solution)/shard_map/ppermute | solution.py:11
  23.2 8.7 %collective-permute-done.5 = bf16[128,768]{1,0:T(8,128)(2,1)S(1)} collective-permute-done((bf16[128,768]{1,0:T(8,128)(2,1)S(1)}, bf16[128,768]{1,0:T(8,128)(2,1)S(1)}, u32[]{:S(2)}, u32[]{:S(2)}) %collective-permute-start.5) | collective-permute-done | bytes 196640 | tf_op jit(solution)/shard_map/ppermute | solution.py:11
  33.8 9.2 %collective-permute-done.8 = bf16[128,768]{1,0:T(8,128)(2,1)S(1)} collective-permute-done((bf16[128,768]{1,0:T(8,128)(2,1)S(1)}, bf16[128,768]{1,0:T(8,128)(2,1)S(1)}, u32[]{:S(2)}, u32[]{:S(2)}) %collective-permute-start.8) | collective-permute-done | bytes 196640 | tf_op jit(solution)/shard_map/ppermute | solution.py:11
  45.7 9.2 %collective-permute-done.11 = bf16[128,768]{1,0:T(8,128)(2,1)S(1)} collective-permute-done((bf16[128,768]{1,0:T(8,128)(2,1)S(1)}, bf16[128,768]{1,0:T(8,128)(2,1)S(1)}, u32[]{:S(2)}, u32[]{:S(2)}) %collective-permute-start.11) | collective-permute-done | bytes 196640 | tf_op jit(solution)/shard_map/ppermute | solution.py:11
  57.5 9.2 %collective-permute-done.14 = bf16[128,768]{1,0:T(8,128)(2,1)S(1)} collective-permute-done((bf16[128,768]{1,0:T(8,128)(2,1)S(1)}, bf16[128,768]{1,0:T(8,128)(2,1)S(1)}, u32[]{:S(2)}, u32[]{:S(2)}) %collective-permute-start.14) | collective-permute-done | bytes 196640 | tf_op jit(solution)/shard_map/ppermute | solution.py:11
  69.4 9.4 %collective-permute-done.17 = bf16[128,768]{1,0:T(8,128)(2,1)} collective-permute-done((bf16[128,768]{1,0:T(8,128)(2,1)S(1)}, bf16[128,768]{1,0:T(8,128)(2,1)}, u32[]{:S(2)}, u32[]{:S(2)}) %collective-permute-start.17) | collective-permute-done | bytes 196640 | tf_op jit(solution)/shard_map/ppermute | solution.py:11
  80.7 56.4 %all-gather.3.cloned.1.call-done = bf16[2048,768]{1,0:T(8,128)(2,1)} async-done(((bf16[32,768]{1,0:T(8,128)(2,1)}), bf16[2048,768]{1,0:T(8,128)(2,1)}) %all-gather.3.cloned.1.call-update) | async-done | bytes 3145744 | tf_op jit(solution)/shard_map/all_gather | solution.py:47
  137.0 4.1 %fusion.31 = (f32[128]{0:T(128)S(1)}, f32[128,2048]{1,0:T(8,128)}) fusion(bf16[128,768]{1,0:T(8,128)(2,1)} %param.3, bf16[2048,768]{1,0:T(8,128)(2,1)} %all-gather.3.cloned.1.call-done), kind=kOutput, calls=%fused_computation.77 | convolution fusion | flops 403177344 | bytes 4391424 | tf_op jit(solution)/shard_map/dot_general | solution.py:17
  141.2 5.2 %collective-permute-start.1 = (f32[128]{0:T(128)S(1)}, f32[128]{0:T(128)S(1)}, u32[]{:S(2)}, u32[]{:S(2)}) collective-permute-start(f32[128]{0:T(128)S(1)} %get-tuple-element.21), channel_id=1, source_target_pairs={{0,1},{1,2},{2,3},{3,4},{4,5},{5,6},{6,7},{7,0},{8,9},{9,10},{10,1... | collective-permute-start | bytes 1544 | tf_op jit(solution)/shard_map/ppermute | solution.py:11
  147.9 110.0 %all-gather.5.cloned.1.call-done = bf16[2048,512]{1,0:T(8,128)(2,1)} async-done(((bf16[32,512]{1,0:T(8,128)(2,1)}), bf16[2048,512]{1,0:T(8,128)(2,1)}) %all-gather.5.cloned.1.call-update) | async-done | bytes 2097168 | tf_op jit(solution)/shard_map/all_gather | solution.py:48
  260.9 4.9 %collective-permute-start = (f32[128,512]{1,0:T(8,128)S(1)}, f32[128,512]{1,0:T(8,128)S(1)}, u32[]{:S(2)}, u32[]{:S(2)}) collective-permute-start(f32[128,512]{1,0:T(8,128)S(1)} %convolution_add_fusion), channel_id=1, source_target_pairs={{0,1},{1,2},{2,3},{3,4},{4,5},{5,6},{6,7},{7,0},{8,9},{9,10},{10,1... | collective-permute-start | bytes 786440 | tf_op jit(solution)/shard_map/ppermute | solution.py:11
  279.9 4.9 %collective-permute-start.4 = (f32[128]{0:T(128)S(1)}, f32[128]{0:T(128)S(1)}, u32[]{:S(2)}, u32[]{:S(2)}) collective-permute-start(f32[128]{0:T(128)S(1)} %max.21), channel_id=1, source_target_pairs={{0,1},{1,2},{2,3},{3,4},{4,5},{5,6},{6,7},{7,0},{8,9},{9,10},{10,1... | collective-permute-start | bytes 1544 | tf_op jit(solution)/shard_map/ppermute | solution.py:11
  288.9 4.5 %collective-permute-start.7 = (f32[128]{0:T(128)S(1)}, f32[128]{0:T(128)S(1)}, u32[]{:S(2)}, u32[]{:S(2)}) collective-permute-start(f32[128]{0:T(128)S(1)} %max.22), channel_id=1, source_target_pairs={{0,1},{1,2},{2,3},{3,4},{4,5},{5,6},{6,7},{7,0},{8,9},{9,10},{10,1... | collective-permute-start | bytes 1544 | tf_op jit(solution)/shard_map/ppermute | solution.py:11
  297.9 4.9 %collective-permute-start.24 = (f32[128]{0:T(128)S(1)}, f32[128]{0:T(128)S(1)}, u32[]{:S(2)}, u32[]{:S(2)}) collective-permute-start(f32[128]{0:T(128)S(1)} %get-tuple-element.15), channel_id=1, source_target_pairs={{0,1},{1,2},{2,3},{3,4},{4,5},{5,6},{6,7},{7,0},{8,9},{9,10},{10,1... | collective-permute-start | bytes 1544 | tf_op jit(solution)/shard_map/ppermute | solution.py:11
  315.3 4.6 %collective-permute-start.13 = (f32[128]{0:T(128)S(1)}, f32[128]{0:T(128)S(1)}, u32[]{:S(2)}, u32[]{:S(2)}) collective-permute-start(f32[128]{0:T(128)S(1)} %max.24), channel_id=1, source_target_pairs={{0,1},{1,2},{2,3},{3,4},{4,5},{5,6},{6,7},{7,0},{8,9},{9,10},{10,1... | collective-permute-start | bytes 1544 | tf_op jit(solution)/shard_map/ppermute | solution.py:11
  325.2 4.5 %collective-permute-start.26 = (f32[128]{0:T(128)S(1)}, f32[128]{0:T(128)S(1)}, u32[]{:S(2)}, u32[]{:S(2)}) collective-permute-start(f32[128]{0:T(128)S(1)} %get-tuple-element.11), channel_id=1, source_target_pairs={{0,1},{1,2},{2,3},{3,4},{4,5},{5,6},{6,7},{7,0},{8,9},{9,10},{10,1... | collective-permute-start | bytes 1544 | tf_op jit(solution)/shard_map/ppermute | solution.py:11
  334.3 4.7 %collective-permute-start.12 = (f32[128,512]{1,0:T(8,128)S(1)}, f32[128,512]{1,0:T(8,128)S(1)}, u32[]{:S(2)}, u32[]{:S(2)}) collective-permute-start(f32[128,512]{1,0:T(8,128)S(1)} %multiply_add_fusion.3), channel_id=1, source_target_pairs={{0,1},{1,2},{2,3},{3,4},{4,5},{5,6},{6,7},{7,0},{8,9},{9,10},{10,1... | collective-permute-start | bytes 786440 | tf_op jit(solution)/shard_map/ppermute | solution.py:11
  339.3 4.2 %collective-permute-start.27 = (f32[128]{0:T(128)S(1)}, f32[128]{0:T(128)S(1)}, u32[]{:S(2)}, u32[]{:S(2)}) collective-permute-start(f32[128]{0:T(128)S(1)} %get-tuple-element.9), channel_id=1, source_target_pairs={{0,1},{1,2},{2,3},{3,4},{4,5},{5,6},{6,7},{7,0},{8,9},{9,10},{10,1... | collective-permute-start | bytes 1544 | tf_op jit(solution)/shard_map/ppermute | solution.py:11
  347.8 3.7 collective-permute-start.15
  351.8 4.8 %collective-permute-start.28 = (f32[128]{0:T(128)S(1)}, f32[128]{0:T(128)S(1)}, u32[]{:S(2)}, u32[]{:S(2)}) collective-permute-start(f32[128]{0:T(128)S(1)} %get-tuple-element.7), channel_id=1, source_target_pairs={{0,1},{1,2},{2,3},{3,4},{4,5},{5,6},{6,7},{7,0},{8,9},{9,10},{10,1... | collective-permute-start | bytes 1544 | tf_op jit(solution)/shard_map/ppermute | solution.py:11
  363.0 9.6 %collective-permute-done.18 = f32[128,512]{1,0:T(8,128)S(1)} collective-permute-done((f32[128,512]{1,0:T(8,128)S(1)}, f32[128,512]{1,0:T(8,128)S(1)}, u32[]{:S(2)}, u32[]{:S(2)}) %collective-permute-start.18) | collective-permute-done | bytes 262176 | tf_op jit(solution)/shard_map/ppermute | solution.py:11
  375.7 4.1 %collective-permute-start.29 = (f32[128]{0:T(128)S(1)}, f32[128]{0:T(128)S(1)}, u32[]{:S(2)}, u32[]{:S(2)}) collective-permute-start(f32[128]{0:T(128)S(1)} %get-tuple-element.5), channel_id=1, source_target_pairs={{0,1},{1,2},{2,3},{3,4},{4,5},{5,6},{6,7},{7,0},{8,9},{9,10},{10,1... | collective-permute-start | bytes 1544 | tf_op jit(solution)/shard_map/ppermute | solution.py:11
  379.8 5.9 %collective-permute-done.29 = f32[128]{0:T(128)S(1)} collective-permute-done((f32[128]{0:T(128)S(1)}, f32[128]{0:T(128)S(1)}, u32[]{:S(2)}, u32[]{:S(2)}) %collective-permute-start.29) | collective-permute-done | bytes 544 | tf_op jit(solution)/shard_map/ppermute | solution.py:11
  (98 shorter events, 80.1 us)
Async XLA Ops:
  6.5 130.5 %all-gather.3.cloned.1.call-start = ((), (), s32[]{:S(2)}) async-start(), calls=%async_computation | async-start | bytes 3194880 | tf_op jit(solution)/shard_map/all_gather | solution.py:47
  7.3 250.6 %all-gather.5.cloned.1.call-start = ((), (), s32[]{:S(2)}) async-start(), calls=%async_computation.1 | async-start | bytes 2129920 | tf_op jit(solution)/shard_map/all_gather | solution.py:48
  8.0 12.5 %collective-permute-start.2 = (bf16[128,768]{1,0:T(8,128)(2,1)}, bf16[128,768]{1,0:T(8,128)(2,1)S(1)}, u32[]{:S(2)}, u32[]{:S(2)}) collective-permute-start(bf16[128,768]{1,0:T(8,128)(2,1)} %param.3), channel_id=1, source_target_pairs={{0,1},{1,2},{2,3},{3,4},{4,5},{5,6},{6,7},{7,0},{8,9},{9,10},{10,1... | collective-permute-start | bytes 589832 | tf_op jit(solution)/shard_map/ppermute | solution.py:11
  78.7 198.8 %collective-permute-start.20 = (bf16[128,768]{1,0:T(8,128)(2,1)}, bf16[128,768]{1,0:T(8,128)(2,1)}, u32[]{:S(2)}, u32[]{:S(2)}) collective-permute-start(bf16[128,768]{1,0:T(8,128)(2,1)} %collective-permute-done.17), channel_id=1, source_target_pairs={{0,1},{1,2},{2,3},{3,4},{4,5},{5,6},{6,7},{7,0},{8,9},{9,10},{10,1... | collective-permute-start | bytes 589832 | tf_op jit(solution)/shard_map/ppermute | solution.py:11
  141.2 138.7 %collective-permute-start.1 = (f32[128]{0:T(128)S(1)}, f32[128]{0:T(128)S(1)}, u32[]{:S(2)}, u32[]{:S(2)}) collective-permute-start(f32[128]{0:T(128)S(1)} %get-tuple-element.21), channel_id=1, source_target_pairs={{0,1},{1,2},{2,3},{3,4},{4,5},{5,6},{6,7},{7,0},{8,9},{9,10},{10,1... | collective-permute-start | bytes 1544 | tf_op jit(solution)/shard_map/ppermute | solution.py:11
  260.9 32.5 %collective-permute-start = (f32[128,512]{1,0:T(8,128)S(1)}, f32[128,512]{1,0:T(8,128)S(1)}, u32[]{:S(2)}, u32[]{:S(2)}) collective-permute-start(f32[128,512]{1,0:T(8,128)S(1)} %convolution_add_fusion), channel_id=1, source_target_pairs={{0,1},{1,2},{2,3},{3,4},{4,5},{5,6},{6,7},{7,0},{8,9},{9,10},{10,1... | collective-permute-start | bytes 786440 | tf_op jit(solution)/shard_map/ppermute | solution.py:11
  265.8 19.2 %collective-permute-start.22 = (f32[128]{0:T(128)S(1)}, f32[128]{0:T(128)S(1)}, u32[]{:S(2)}, u32[]{:S(2)}) collective-permute-start(f32[128]{0:T(128)S(1)} %get-tuple-element.19), channel_id=1, source_target_pairs={{0,1},{1,2},{2,3},{3,4},{4,5},{5,6},{6,7},{7,0},{8,9},{9,10},{10,1... | collective-permute-start | bytes 1544 | tf_op jit(solution)/shard_map/ppermute | solution.py:11
  285.1 12.9 %collective-permute-start.23 = (f32[128]{0:T(128)S(1)}, f32[128]{0:T(128)S(1)}, u32[]{:S(2)}, u32[]{:S(2)}) collective-permute-start(f32[128]{0:T(128)S(1)} %get-tuple-element.17), channel_id=1, source_target_pairs={{0,1},{1,2},{2,3},{3,4},{4,5},{5,6},{6,7},{7,0},{8,9},{9,10},{10,1... | collective-permute-start | bytes 1544 | tf_op jit(solution)/shard_map/ppermute | solution.py:11
  288.9 13.9 %collective-permute-start.7 = (f32[128]{0:T(128)S(1)}, f32[128]{0:T(128)S(1)}, u32[]{:S(2)}, u32[]{:S(2)}) collective-permute-start(f32[128]{0:T(128)S(1)} %max.22), channel_id=1, source_target_pairs={{0,1},{1,2},{2,3},{3,4},{4,5},{5,6},{6,7},{7,0},{8,9},{9,10},{10,1... | collective-permute-start | bytes 1544 | tf_op jit(solution)/shard_map/ppermute | solution.py:11
  294.5 12.6 %collective-permute-start.3 = (f32[128,512]{1,0:T(8,128)S(1)}, f32[128,512]{1,0:T(8,128)S(1)}, u32[]{:S(2)}, u32[]{:S(2)}) collective-permute-start(f32[128,512]{1,0:T(8,128)S(1)} %multiply_add_fusion.6), channel_id=1, source_target_pairs={{0,1},{1,2},{2,3},{3,4},{4,5},{5,6},{6,7},{7,0},{8,9},{9,10},{10,1... | collective-permute-start | bytes 786440 | tf_op jit(solution)/shard_map/ppermute | solution.py:11
  297.9 13.6 %collective-permute-start.24 = (f32[128]{0:T(128)S(1)}, f32[128]{0:T(128)S(1)}, u32[]{:S(2)}, u32[]{:S(2)}) collective-permute-start(f32[128]{0:T(128)S(1)} %get-tuple-element.15), channel_id=1, source_target_pairs={{0,1},{1,2},{2,3},{3,4},{4,5},{5,6},{6,7},{7,0},{8,9},{9,10},{10,1... | collective-permute-start | bytes 1544 | tf_op jit(solution)/shard_map/ppermute | solution.py:11
  302.8 12.5 %collective-permute-start.10 = (f32[128]{0:T(128)S(1)}, f32[128]{0:T(128)S(1)}, u32[]{:S(2)}, u32[]{:S(2)}) collective-permute-start(f32[128]{0:T(128)S(1)} %max.23), channel_id=1, source_target_pairs={{0,1},{1,2},{2,3},{3,4},{4,5},{5,6},{6,7},{7,0},{8,9},{9,10},{10,1... | collective-permute-start | bytes 1544 | tf_op jit(solution)/shard_map/ppermute | solution.py:11
  308.2 11.9 %collective-permute-start.6 = (f32[128,512]{1,0:T(8,128)S(1)}, f32[128,512]{1,0:T(8,128)S(1)}, u32[]{:S(2)}, u32[]{:S(2)}) collective-permute-start(f32[128,512]{1,0:T(8,128)S(1)} %multiply_add_fusion.5), channel_id=1, source_target_pairs={{0,1},{1,2},{2,3},{3,4},{4,5},{5,6},{6,7},{7,0},{8,9},{9,10},{10,1... | collective-permute-start | bytes 786440 | tf_op jit(solution)/shard_map/ppermute | solution.py:11
  311.6 13.5 %collective-permute-start.25 = (f32[128]{0:T(128)S(1)}, f32[128]{0:T(128)S(1)}, u32[]{:S(2)}, u32[]{:S(2)}) collective-permute-start(f32[128]{0:T(128)S(1)} %get-tuple-element.13), channel_id=1, source_target_pairs={{0,1},{1,2},{2,3},{3,4},{4,5},{5,6},{6,7},{7,0},{8,9},{9,10},{10,1... | collective-permute-start | bytes 1544 | tf_op jit(solution)/shard_map/ppermute | solution.py:11
  315.3 14.3 %collective-permute-start.13 = (f32[128]{0:T(128)S(1)}, f32[128]{0:T(128)S(1)}, u32[]{:S(2)}, u32[]{:S(2)}) collective-permute-start(f32[128]{0:T(128)S(1)} %max.24), channel_id=1, source_target_pairs={{0,1},{1,2},{2,3},{3,4},{4,5},{5,6},{6,7},{7,0},{8,9},{9,10},{10,1... | collective-permute-start | bytes 1544 | tf_op jit(solution)/shard_map/ppermute | solution.py:11
  321.2 11.9 %collective-permute-start.9 = (f32[128,512]{1,0:T(8,128)S(1)}, f32[128,512]{1,0:T(8,128)S(1)}, u32[]{:S(2)}, u32[]{:S(2)}) collective-permute-start(f32[128,512]{1,0:T(8,128)S(1)} %multiply_add_fusion.4), channel_id=1, source_target_pairs={{0,1},{1,2},{2,3},{3,4},{4,5},{5,6},{6,7},{7,0},{8,9},{9,10},{10,1... | collective-permute-start | bytes 786440 | tf_op jit(solution)/shard_map/ppermute | solution.py:11
  325.2 14.1 %collective-permute-start.26 = (f32[128]{0:T(128)S(1)}, f32[128]{0:T(128)S(1)}, u32[]{:S(2)}, u32[]{:S(2)}) collective-permute-start(f32[128]{0:T(128)S(1)} %get-tuple-element.11), channel_id=1, source_target_pairs={{0,1},{1,2},{2,3},{3,4},{4,5},{5,6},{6,7},{7,0},{8,9},{9,10},{10,1... | collective-permute-start | bytes 1544 | tf_op jit(solution)/shard_map/ppermute | solution.py:11
  329.7 13.9 %collective-permute-start.16 = (f32[128]{0:T(128)S(1)}, f32[128]{0:T(128)S(1)}, u32[]{:S(2)}, u32[]{:S(2)}) collective-permute-start(f32[128]{0:T(128)S(1)} %max.25), channel_id=1, source_target_pairs={{0,1},{1,2},{2,3},{3,4},{4,5},{5,6},{6,7},{7,0},{8,9},{9,10},{10,1... | collective-permute-start | bytes 1544 | tf_op jit(solution)/shard_map/ppermute | solution.py:11
  334.3 12.4 %collective-permute-start.12 = (f32[128,512]{1,0:T(8,128)S(1)}, f32[128,512]{1,0:T(8,128)S(1)}, u32[]{:S(2)}, u32[]{:S(2)}) collective-permute-start(f32[128,512]{1,0:T(8,128)S(1)} %multiply_add_fusion.3), channel_id=1, source_target_pairs={{0,1},{1,2},{2,3},{3,4},{4,5},{5,6},{6,7},{7,0},{8,9},{9,10},{10,1... | collective-permute-start | bytes 786440 | tf_op jit(solution)/shard_map/ppermute | solution.py:11
  339.3 12.5 %collective-permute-start.27 = (f32[128]{0:T(128)S(1)}, f32[128]{0:T(128)S(1)}, u32[]{:S(2)}, u32[]{:S(2)}) collective-permute-start(f32[128]{0:T(128)S(1)} %get-tuple-element.9), channel_id=1, source_target_pairs={{0,1},{1,2},{2,3},{3,4},{4,5},{5,6},{6,7},{7,0},{8,9},{9,10},{10,1... | collective-permute-start | bytes 1544 | tf_op jit(solution)/shard_map/ppermute | solution.py:11
  343.5 13.0 %collective-permute-start.19 = (f32[128]{0:T(128)S(1)}, f32[128]{0:T(128)S(1)}, u32[]{:S(2)}, u32[]{:S(2)}) collective-permute-start(f32[128]{0:T(128)S(1)} %max.26), channel_id=1, source_target_pairs={{0,1},{1,2},{2,3},{3,4},{4,5},{5,6},{6,7},{7,0},{8,9},{9,10},{10,1... | collective-permute-start | bytes 1544 | tf_op jit(solution)/shard_map/ppermute | solution.py:11
  347.8 11.9 %collective-permute-start.15 = (f32[128,512]{1,0:T(8,128)S(1)}, f32[128,512]{1,0:T(8,128)S(1)}, u32[]{:S(2)}, u32[]{:S(2)}) collective-permute-start(f32[128,512]{1,0:T(8,128)S(1)} %multiply_add_fusion.2), channel_id=1, source_target_pairs={{0,1},{1,2},{2,3},{3,4},{4,5},{5,6},{6,7},{7,0},{8,9},{9,10},{10,1... | collective-permute-start | bytes 786440 | tf_op jit(solution)/shard_map/ppermute | solution.py:11
  360.8 11.9 %collective-permute-start.18 = (f32[128,512]{1,0:T(8,128)S(1)}, f32[128,512]{1,0:T(8,128)S(1)}, u32[]{:S(2)}, u32[]{:S(2)}) collective-permute-start(f32[128,512]{1,0:T(8,128)S(1)} %multiply_add_fusion.1), channel_id=1, source_target_pairs={{0,1},{1,2},{2,3},{3,4},{4,5},{5,6},{6,7},{7,0},{8,9},{9,10},{10,1... | collective-permute-start | bytes 786440 | tf_op jit(solution)/shard_map/ppermute | solution.py:11
  373.8 11.9 %collective-permute-start.21 = (f32[128,512]{1,0:T(8,128)S(1)}, f32[128,512]{1,0:T(8,128)S(1)}, u32[]{:S(2)}, u32[]{:S(2)}) collective-permute-start(f32[128,512]{1,0:T(8,128)S(1)} %multiply_add_fusion), channel_id=1, source_target_pairs={{0,1},{1,2},{2,3},{3,4},{4,5},{5,6},{6,7},{7,0},{8,9},{9,10},{10,1... | collective-permute-start | bytes 786440 | tf_op jit(solution)/shard_map/ppermute | solution.py:11
  (16 other events, 236.1 us)
Sparse Core Ops, SparseCore 0:
  9.5 127.4 all-gather.2
  139.2 118.6 all-gather.4
where the time goes:
time: 394 us; the launch traced here: 393 us
  waiting for transfers between devices  242 us (61%)
  starting transfers between devices  105 us (27%)
  matrix products  25.5 us (6%)
  between operations  14 us (4%)
  other arithmetic  4.44 us (1%)
    all_gather x1, waiting for transfers between devices, shards(): lax.all_gather(labels, 'blk', axis=0, tiled=True)  110 us
    ppermute x30, starting transfers between devices, shifted(): lax.ppermute(value, axis, [(i, (i + by) % devices) for i in range(devices)])  105 us
    ppermute x30, waiting for transfers between devices, shifted(): lax.ppermute(value, axis, [(i, (i + by) % devices) for i in range(devices)])  74.4 us
    all_gather x1, waiting for transfers between devices, shards(): lax.all_gather(keys, 'blk', axis=0, tiled=True)  56.4 us
    dot_general x8, matrix products, update(): lax.dot_general(visiting, row_keys, (((1,), (1,)), ((), ())), preferred_e...  14.7 us
    dot_general x8, matrix products, update(): jnp.dot(weights, label_values, preferred_element_type=jnp.float32, precis...  10.8 us
  transfers between devices with their start and end apart: 32, of which 15 were waited for; matrix products, arithmetic and copies ran while one was open for 7% of the time, Pallas kernels for 0%

commit v1 on v0

v1 whole, which is shorter than its diff:
```python
import functools
import math

import jax
import jax.numpy as jnp
from jax import lax
from jax.experimental import pallas as pl
from jax.experimental.pallas import tpu as pltpu
from jax.sharding import Mesh
from jax.sharding import PartitionSpec as P

AXES = ("x_lo", "z_hi", "z_lo", "core", "y", "x_hi")
SIZES = (2, 8, 2, 2, 4, 2)
Z = ("z_hi", "z_lo")
PLANE = ("x_lo", "y", "x_hi")
EXTRA = 16
STEP = 512


def copies(value, count):
    rows, width = value.shape
    return jnp.broadcast_to(value[None], (count, rows, width)).reshape(count * rows, width)


def exchange(value, axes):
    return lax.all_to_all(value, axes, 0, 0, tiled=True)


def shifted(value, axes, by):
    devices = lax.axis_size(axes)
    return lax.ppermute(value, axes, [(i, (i + by) % devices) for i in range(devices)])


def classify(sharpness, *refs):
    *row_refs, queries_ref, out_ref, rows_ref, panel_ref, labels_ref, semaphores = refs
    features = queries_ref.shape[1]
    panels = queries_ref.shape[0] // STEP
    classes, wide = out_ref.shape[1] - EXTRA, out_ref.shape[2]
    fetches, at = [], 0
    for ref in row_refs:
        fetches.append((ref, rows_ref.at[at : at + ref.shape[0], :]))
        at += ref.shape[0]
    for panel in range(panels):
        part = slice(panel * STEP, (panel + 1) * STEP)
        fetches.append((queries_ref.at[part, :], panel_ref.at[part, :]))
    fetches = [
        pltpu.make_async_copy(source, target, semaphores.at[index])
        for index, (source, target) in enumerate(fetches)
    ]
    for fetch in fetches:
        fetch.start()
    for fetch in fetches[: len(row_refs)]:
        fetch.wait()

    def products(panel):
        fetches[len(row_refs) + panel].wait()
        return lax.dot_general(
            rows_ref[:, :features],
            panel_ref[panel * STEP : (panel + 1) * STEP, :],
            (((1,), (1,)), ((), ())),
            preferred_element_type=jnp.float32,
        )

    rate = sharpness * math.log2(math.e)
    row = lax.broadcasted_iota(jnp.int32, (EXTRA, STEP), 0)
    later = products(0)
    labels_ref[...] = rows_ref[:, features:].T
    for panel in range(panels):
        now, later = later, products(panel + 1) if panel + 1 < panels else None
        top = jnp.max(now, axis=0, keepdims=True)
        weights = jnp.exp2((now - top) * rate)
        total = jnp.sum(weights, axis=0, keepdims=True)
        weighted = jnp.dot(
            labels_ref[...], weights.astype(jnp.bfloat16), preferred_element_type=jnp.float32
        )
        mean = (weighted * (1.0 / total)).astype(jnp.bfloat16)
        level = top * sharpness + jnp.log(total)
        first = level.astype(jnp.bfloat16).astype(jnp.float32)
        second = (level - first).astype(jnp.bfloat16).astype(jnp.float32)
        third = level - first - second
        parts = jnp.where(
            row == 0, first, jnp.where(row == 1, second, jnp.where(row == 2, third, 0.0))
        ).astype(jnp.bfloat16)
        for column in range(0, STEP, wide):
            block = (panel * STEP + column) // wide
            out_ref[block, :classes, :] = mean[:, column : column + wide]
            out_ref[block, classes:, :] = parts[:, column : column + wide]


def combine(parts_ref, out_ref):
    sources = parts_ref.shape[0]
    classes = parts_ref.shape[1] - EXTRA
    levels = [
        jnp.sum(parts_ref[source, classes:, :].astype(jnp.float32), axis=0, keepdims=True)
        for source in range(sources)
    ]
    top = functools.reduce(jnp.maximum, levels)
    shares = [jnp.exp(level - top) for level in levels]
    scale = 1.0 / sum(shares)
    shares = [share * scale for share in shares]
    for at in range(0, classes, 128):
        mean = sum(
            shares[source] * parts_ref[source, at : at + 128, :].astype(jnp.float32)
            for source in range(sources)
        )
        out_ref[:, at : at + 128] = mean.T.astype(out_ref.dtype)


def shards(queries, keys, labels):
    count, features = queries.shape
    classes = labels.shape[1]
    plane = lax.axis_size(PLANE)
    sharpness = 2.5 / math.sqrt(features)

    panel = exchange(copies(queries, plane), PLANE)

    rows = jnp.concatenate([keys, labels], axis=1)
    same = lax.all_gather(rows, "z_hi", axis=0, tiled=True)
    half = same.shape[0] // 2
    other = jnp.concatenate([shifted(same[:half], Z, 1), shifted(same[half:], Z, -1)], axis=0)
    row_parts = [same, shifted(same, "core", 1), other, shifted(other, "core", 1)]

    held = sum(part.shape[0] for part in row_parts)
    anywhere = pl.BlockSpec(memory_space=pltpu.HBM)
    parts = pl.pallas_call(
        functools.partial(classify, sharpness),
        in_specs=[anywhere] * (len(row_parts) + 1),
        out_specs=pl.BlockSpec(memory_space=pltpu.VMEM),
        out_shape=jax.ShapeDtypeStruct((plane, classes + EXTRA, count), jnp.bfloat16),
        scratch_shapes=[
            pltpu.VMEM((held, features + classes), jnp.bfloat16),
            pltpu.VMEM((plane * count, features), jnp.bfloat16),
            pltpu.VMEM((classes, held), jnp.bfloat16),
            pltpu.SemaphoreType.DMA((len(row_parts) + plane * count // STEP,)),
        ],
        compiler_params=pltpu.CompilerParams(vmem_limit_bytes=58 * 2**20),
        cost_estimate=pl.CostEstimate(
            flops=2 * plane * count * held * (features + classes),
            bytes_accessed=9 * 2**20,
            transcendentals=plane * count * held,
        ),
        name="classify",
    )(*row_parts, panel)
    parts = exchange(parts, PLANE)
    return pl.pallas_call(
        combine,
        out_shape=jax.ShapeDtypeStruct((count, classes), jnp.bfloat16),
        compiler_params=pltpu.CompilerParams(vmem_limit_bytes=20 * 2**20),
        cost_estimate=pl.CostEstimate(
            flops=2 * plane * count * classes, bytes_accessed=3 * 2**20, transcendentals=0
        ),
        name="combine",
    )(parts)


def solution(mesh):
    chips = Mesh(mesh.devices.reshape(SIZES), AXES)
    placed = P(AXES, None)
    return jax.shard_map(
        shards, mesh=chips, in_specs=(placed, placed, placed), out_specs=placed, check_vma=False
    )
```

time: 394 us -> 114 us (0.29)
  the two profiles are of different devices: /device:TPU:32 before, /device:TPU:1 now
where the time goes in v1:
time: 114 us
  blocking collectives  69.9 us (61%)
  starting transfers between devices  26.3 us (23%)
  Pallas kernels  11.1 us (10%)
  local copies, waits for them, and re-layouts  5.43 us (5%)
    all_to_all x1, blocking collectives, exchange(): return lax.all_to_all(value, axes, 0, 0, tiled=True)  35.9 us
    all_gather x1, blocking collectives, shards(): same = lax.all_gather(rows, 'z_hi', axis=0, tiled=True)  33.9 us
    ppermute x4, starting transfers between devices, shifted(): lax.ppermute(value, axes, [(i, (i + by) % devices) for i in range(devices)])  18.6 us
    pallas_call x1, Pallas kernels, shards(): pl.pallas_call(functools.partial(classify, sharpness), in_specs=[anywhere...  9.89 us
    all_to_all x1, starting transfers between devices, exchange(): return lax.all_to_all(value, axes, 0, 0, tiled=True)  7.72 us
    broadcast_in_dim x1, local copies, waits for them, and re-layouts, copies(): jnp.broadcast_to(value[None], (count, rows, width))  2.86 us
    unnamed x13, local copies, waits for them, and re-layouts  2.51 us
  transfers between devices with their start and end apart: 5, of which 1 were waited for; matrix products, arithmetic and copies ran while one was open for 0% of the time, Pallas kernels for 0%

profile of v1, /device:TPU:1, one launch (start us, length us, event | category | flops | bytes accessed | tf_op | source)
XLA Modules:
  0.0 113.8 jit_solution(13903544603660970419)
XLA Ops:
  0.0 2.9 %broadcast_in_dim.2 = bf16[16,128,768]{2,1,0:T(8,128)(2,1)} broadcast(bf16[128,768]{1,0:T(8,128)(2,1)} %param.3), dimensions={1,2} | broadcast | bytes 3342336 | tf_op jit(solution)/shard_map/broadcast_in_dim | solution.py:22
  2.9 0.0 copy-start.3
  2.9 7.7 %all-to-all-start = ((bf16[16,128,768]{2,1,0:T(8,128)(2,1)}), bf16[16,128,768]{2,1,0:T(8,128)(2,1)S(1)}, u32[]{:S(2)}, u32[]{:S(2)}) async-start(bf16[16,128,768]{2,1,0:T(8,128)(2,1)} %broadcast_in_dim.2), calls=%async_computation | async-start | bytes 6291456 | tf_op jit(solution)/shard_map/all_to_all | solution.py:26
  10.6 0.0 copy-done.3
  10.6 0.0 copy-done.4
  10.6 33.9 %all_gather.3.refs_0_ = bf16[256,1280]{1,0:T(8,128)(2,1)S(1)} all-gather(bf16[32,1280]{1,0:T(8,128)(2,1)S(1)} %pad_maximum_fusion), channel_id=1, replica_groups=mesh['x_lo'=2,'z_hi'=8,'z_lo'=2,'core'=2,'y'=4,'x_hi'=2] {'z_hi'}, dimensions={0}, use_global_device_ids=true | all-gather | bytes 737280 | tf_op jit(solution)/shard_map/all_gather | solution.py:118
  44.6 2.6 %collective-permute-start.1 = (bf16[128,1280]{1,0:T(8,128)(2,1)S(1)}, bf16[128,1280]{1,0:T(8,128)(2,1)S(1)}, u32[]{:S(2)}, u32[]{:S(2)}) collective-permute-start(bf16[128,1280]{1,0:T(8,128)(2,1)S(1)} %get-tuple-element.6), channel_id=1, source_target_pairs={{0,16},{16,32},{32,48},{48,64},{64,80},{80,96},{96,112},{112,128},... | collective-permute-start | bytes 983048 | tf_op jit(solution)/shard_map/ppermute | solution.py:31
  47.1 3.9 %collective-permute-start.2 = (bf16[128,1280]{1,0:T(8,128)(2,1)S(1)}, bf16[128,1280]{1,0:T(8,128)(2,1)S(1)}, u32[]{:S(2)}, u32[]{:S(2)}) collective-permute-start(bf16[128,1280]{1,0:T(8,128)(2,1)S(1)} %get-tuple-element.5), channel_id=1, source_target_pairs={{0,240},{16,0},{32,16},{48,32},{64,48},{80,64},{96,80},{112,96},{1... | collective-permute-start | bytes 983048 | tf_op jit(solution)/shard_map/ppermute | solution.py:31
  51.1 7.6 %collective-permute-start = (bf16[256,1280]{1,0:T(8,128)(2,1)S(1)}, bf16[256,1280]{1,0:T(8,128)(2,1)S(1)}, u32[]{:S(2)}, u32[]{:S(2)}) collective-permute-start(bf16[256,1280]{1,0:T(8,128)(2,1)S(1)} %all_gather.3.refs_0_), channel_id=1, source_target_pairs={{0,8},{8,0},{1,9},{9,1},{2,10},{10,2},{3,11},{11,3},{4,12},{12,4},... | collective-permute-start | bytes 1966088 | tf_op jit(solution)/shard_map/ppermute | solution.py:31
  58.7 0.0 collective-permute-done.1
  58.7 0.0 collective-permute-done.2
  58.8 0.0 copy-start.2
  58.8 4.5 %collective-permute-start.3 = (bf16[256,1280]{1,0:T(8,128)(2,1)S(1)}, bf16[256,1280]{1,0:T(8,128)(2,1)}, u32[]{:S(2)}, u32[]{:S(2)}) collective-permute-start(bf16[256,1280]{1,0:T(8,128)(2,1)S(1)} %constant_dynamic-update-slice_fusion.refs_2_), channel_id=1, source_target_pairs={{0,8},{8,0},{1,9},{9,1},{2,10},{10,2},{3,11},{11,3},{4,12},{12,4},... | collective-permute-start | bytes 1966088 | tf_op jit(solution)/shard_map/ppermute | solution.py:31
  63.3 0.0 collective-permute-done.refs_1_
  63.3 0.0 copy-done.1
  63.3 0.0 copy-done.2
  63.3 0.0 copy-start.5
  63.3 0.8 copy-done.5
  64.2 0.9 collective-permute-done.3.refs_3_
  65.1 0.0 all-to-all-done
  65.1 1.6 %copy-done = bf16[16,128,768]{2,1,0:T(8,128)(2,1)} copy-done((bf16[16,128,768]{2,1,0:T(8,128)(2,1)}, bf16[16,128,768]{2,1,0:T(8,128)(2,1)S(1)}, u32[]{:S(2)}) %copy-start) | copy-done | bytes 3145752
  66.8 9.9 %classify.1 = bf16[16,528,128]{2,1,0:T(8,128)(2,1)} custom-call(bf16[256,1280]{1,0:T(8,128)(2,1)} %copy-done.1, bf16[256,1280]{1,0:T(8,128)(2,1)} %copy-done.5, bf16[256,1280]{1,0:T(8,128)(2,1)} %copy-done.2, bf16[256,1280]{1,0:T(8,128)(2,1)} %collective-permute-done.3.refs_3_, bf16[2048,768]{1,0:T(8,128)(2,1)} %bitcast.1), custom_call_target="tpu_custom_call" | custom-call | flops 5368709120 | bytes 9437184 | tf_op jit(solution)/shard_map/classify/pallas_call | solution.py:125
  76.7 35.9 %all_to_all.13.parts_ref = bf16[16,528,128]{2,1,0:T(8,128)(2,1)S(1)} all-to-all(bf16[16,528,128]{2,1,0:T(8,128)(2,1)} %classify.1), channel_id=1, replica_groups=mesh['x_lo'=2,'z_hi'=8,'z_lo'=2,'core'=2,'y'=4,'x_hi'=2] {'x_lo','y','x_..., dimensions={0} | all-to-all | bytes 4325376 | tf_op jit(solution)/shard_map/all_to_all | solution.py:26
  112.6 1.2 %combine.1 = bf16[128,512]{1,0:T(8,128)(2,1)} custom-call(bf16[16,528,128]{2,1,0:T(8,128)(2,1)S(1)} %all_to_all.13.parts_ref), custom_call_target="tpu_custom_call" | custom-call | flops 2097152 | bytes 3145728 | tf_op jit(solution)/shard_map/combine/pallas_call | solution.py:145
  (7 shorter events, 0.1 us)
Async XLA Ops:
  2.9 7.7 %copy-start.3 = (bf16[32,768]{1,0:T(8,128)(2,1)S(1)}, bf16[32,768]{1,0:T(8,128)(2,1)}, u32[]{:S(2)}) copy-start(bf16[32,768]{1,0:T(8,128)(2,1)} %param.4) | copy-start | bytes 147460
  2.9 7.7 %copy-start.4 = (bf16[32,512]{1,0:T(8,128)(2,1)S(1)}, bf16[32,512]{1,0:T(8,128)(2,1)}, u32[]{:S(2)}) copy-start(bf16[32,512]{1,0:T(8,128)(2,1)} %param.5) | copy-start | bytes 98308
  2.9 62.3 %all-to-all-start = ((bf16[16,128,768]{2,1,0:T(8,128)(2,1)}), bf16[16,128,768]{2,1,0:T(8,128)(2,1)S(1)}, u32[]{:S(2)}, u32[]{:S(2)}) async-start(bf16[16,128,768]{2,1,0:T(8,128)(2,1)} %broadcast_in_dim.2), calls=%async_computation | async-start | bytes 6291456 | tf_op jit(solution)/shard_map/all_to_all | solution.py:26
  44.5 18.8 %copy-start.1 = (bf16[256,1280]{1,0:T(8,128)(2,1)}, bf16[256,1280]{1,0:T(8,128)(2,1)S(1)}, u32[]{:S(2)}) copy-start(bf16[256,1280]{1,0:T(8,128)(2,1)S(1)} %all_gather.3.refs_0_) | copy-start | bytes 1966084
  44.6 14.1 %collective-permute-start.1 = (bf16[128,1280]{1,0:T(8,128)(2,1)S(1)}, bf16[128,1280]{1,0:T(8,128)(2,1)S(1)}, u32[]{:S(2)}, u32[]{:S(2)}) collective-permute-start(bf16[128,1280]{1,0:T(8,128)(2,1)S(1)} %get-tuple-element.6), channel_id=1, source_target_pairs={{0,16},{16,32},{32,48},{48,64},{64,80},{80,96},{96,112},{112,128},... | collective-permute-start | bytes 983048 | tf_op jit(solution)/shard_map/ppermute | solution.py:31
  47.1 11.6 %collective-permute-start.2 = (bf16[128,1280]{1,0:T(8,128)(2,1)S(1)}, bf16[128,1280]{1,0:T(8,128)(2,1)S(1)}, u32[]{:S(2)}, u32[]{:S(2)}) collective-permute-start(bf16[128,1280]{1,0:T(8,128)(2,1)S(1)} %get-tuple-element.5), channel_id=1, source_target_pairs={{0,240},{16,0},{32,16},{48,32},{64,48},{80,64},{96,80},{112,96},{1... | collective-permute-start | bytes 983048 | tf_op jit(solution)/shard_map/ppermute | solution.py:31
  51.1 12.2 %collective-permute-start = (bf16[256,1280]{1,0:T(8,128)(2,1)S(1)}, bf16[256,1280]{1,0:T(8,128)(2,1)S(1)}, u32[]{:S(2)}, u32[]{:S(2)}) collective-permute-start(bf16[256,1280]{1,0:T(8,128)(2,1)S(1)} %all_gather.3.refs_0_), channel_id=1, source_target_pairs={{0,8},{8,0},{1,9},{9,1},{2,10},{10,2},{3,11},{11,3},{4,12},{12,4},... | collective-permute-start | bytes 1966088 | tf_op jit(solution)/shard_map/ppermute | solution.py:31
  58.8 4.5 %copy-start.2 = (bf16[256,1280]{1,0:T(8,128)(2,1)}, bf16[256,1280]{1,0:T(8,128)(2,1)S(1)}, u32[]{:S(2)}) copy-start(bf16[256,1280]{1,0:T(8,128)(2,1)S(1)} %constant_dynamic-update-slice_fusion.refs_2_) | copy-start | bytes 1966084
  58.8 6.3 %collective-permute-start.3 = (bf16[256,1280]{1,0:T(8,128)(2,1)S(1)}, bf16[256,1280]{1,0:T(8,128)(2,1)}, u32[]{:S(2)}, u32[]{:S(2)}) collective-permute-start(bf16[256,1280]{1,0:T(8,128)(2,1)S(1)} %constant_dynamic-update-slice_fusion.refs_2_), channel_id=1, source_target_pairs={{0,8},{8,0},{1,9},{9,1},{2,10},{10,2},{3,11},{11,3},{4,12},{12,4},... | collective-permute-start | bytes 1966088 | tf_op jit(solution)/shard_map/ppermute | solution.py:31
  63.3 0.9 copy-start.5
  65.1 1.6 %copy-start = (bf16[16,128,768]{2,1,0:T(8,128)(2,1)}, bf16[16,128,768]{2,1,0:T(8,128)(2,1)S(1)}, u32[]{:S(2)}) copy-start(bf16[16,128,768]{2,1,0:T(8,128)(2,1)S(1)} %all-to-all-done) | copy-start | bytes 9437188

commit v2 on v1

v2 whole, which is shorter than its diff:
```python
import functools
import math

import jax
import jax.numpy as jnp
from jax import lax
from jax.experimental import pallas as pl
from jax.experimental.pallas import tpu as pltpu
from jax.sharding import Mesh
from jax.sharding import PartitionSpec as P

AXES = ("x_lo", "z_hi", "z_lo", "core", "y", "x_hi")
SIZES = (2, 8, 2, 2, 4, 2)
Z = ("z_hi", "z_lo")
PLANE = ("x_lo", "y", "x_hi")
EXTRA = 16
STEP = 512


def copies(value, count):
    rows, width = value.shape
    return jnp.broadcast_to(value[None], (count, rows, width)).reshape(count * rows, width)


def exchange(value, axes):
    return lax.all_to_all(value, axes, 0, 0, tiled=True)


def shifted(value, axes, by):
    devices = lax.axis_size(axes)
    return lax.ppermute(value, axes, [(i, (i + by) % devices) for i in range(devices)])


def classify(sharpness, *refs):
    *row_refs, queries_ref, parts_ref = refs[:-5]
    panel_ref, labels_ref, out_ref, arrivals, departures = refs[-5:]
    features = queries_ref.shape[1]
    panels = queries_ref.shape[0] // STEP
    blocks, classes, wide = out_ref.shape
    classes -= EXTRA
    per_panel = blocks // panels
    held = row_refs[0].shape[0]

    fetches = []
    for panel in range(panels):
        part = slice(panel * STEP, (panel + 1) * STEP)
        fetches.append(
            pltpu.make_async_copy(
                queries_ref.at[part, :], panel_ref.at[part, :], arrivals.at[panel]
            )
        )
    for fetch in fetches:
        fetch.start()
    for index, ref in enumerate(row_refs):
        labels_ref[:, index * held : (index + 1) * held] = ref[:, features:].T

    def products(panel):
        fetches[panel].wait()
        return [
            lax.dot_general(
                ref[:, :features],
                panel_ref[panel * STEP : (panel + 1) * STEP, :],
                (((1,), (1,)), ((), ())),
                preferred_element_type=jnp.float32,
            )
            for ref in row_refs
        ]

    rate = sharpness * math.log2(math.e)
    row = lax.broadcasted_iota(jnp.int32, (EXTRA, STEP), 0)
    later = products(0)
    sends = []
    for panel in range(panels):
        now, later = later, products(panel + 1) if panel + 1 < panels else None
        top = functools.reduce(jnp.maximum, [jnp.max(part, axis=0, keepdims=True) for part in now])
        weights = [jnp.exp2((part - top) * rate) for part in now]
        total = sum(jnp.sum(part, axis=0, keepdims=True) for part in weights)
        weighted = sum(
            jnp.dot(
                labels_ref[:, index * held : (index + 1) * held],
                part.astype(jnp.bfloat16),
                preferred_element_type=jnp.float32,
            )
            for index, part in enumerate(weights)
        )
        mean = (weighted * (1.0 / total)).astype(jnp.bfloat16)
        level = top * sharpness + jnp.log(total)
        first = level.astype(jnp.bfloat16).astype(jnp.float32)
        second = (level - first).astype(jnp.bfloat16).astype(jnp.float32)
        third = level - first - second
        parts = jnp.where(
            row == 0, first, jnp.where(row == 1, second, jnp.where(row == 2, third, 0.0))
        ).astype(jnp.bfloat16)
        for index in range(per_panel):
            block = panel * per_panel + index
            out_ref[block, :classes, :] = mean[:, index * wide : (index + 1) * wide]
            out_ref[block, classes:, :] = parts[:, index * wide : (index + 1) * wide]
        done = slice(panel * per_panel, (panel + 1) * per_panel)
        send = pltpu.make_async_copy(out_ref.at[done], parts_ref.at[done], departures.at[panel])
        send.start()
        sends.append(send)
    for send in sends:
        send.wait()


def combine(parts_ref, out_ref):
    sources = parts_ref.shape[0]
    classes = parts_ref.shape[1] - EXTRA
    levels = [
        jnp.sum(parts_ref[source, classes:, :].astype(jnp.float32), axis=0, keepdims=True)
        for source in range(sources)
    ]
    top = functools.reduce(jnp.maximum, levels)
    shares = [jnp.exp(level - top) for level in levels]
    scale = 1.0 / sum(shares)
    shares = [share * scale for share in shares]
    for at in range(0, classes, 128):
        mean = sum(
            shares[source] * parts_ref[source, at : at + 128, :].astype(jnp.float32)
            for source in range(sources)
        )
        out_ref[:, at : at + 128] = mean.T.astype(out_ref.dtype)


def shards(queries, keys, labels):
    count, features = queries.shape
    classes = labels.shape[1]
    plane = lax.axis_size(PLANE)
    sharpness = 2.5 / math.sqrt(features)

    anywhere = pl.BlockSpec(memory_space=pltpu.HBM)
    inside = pl.BlockSpec(memory_space=pltpu.VMEM)
    panel = exchange(copies(queries, plane), PLANE)

    rows = jnp.concatenate([keys, labels], axis=1)
    same = lax.all_gather(rows, "z_hi", axis=0, tiled=True)
    middle = same.shape[0] // 2
    other = jnp.concatenate([shifted(same[:middle], Z, 1), shifted(same[middle:], Z, -1)], axis=0)
    parts = [same, shifted(same, "core", 1), other, shifted(other, "core", 1)]

    held = sum(part.shape[0] for part in parts)
    blocks = (plane, classes + EXTRA, count)
    parts = pl.pallas_call(
        functools.partial(classify, sharpness),
        in_specs=[inside] * len(parts) + [anywhere],
        out_specs=anywhere,
        out_shape=jax.ShapeDtypeStruct(blocks, jnp.bfloat16),
        scratch_shapes=[
            pltpu.VMEM((plane * count, features), jnp.bfloat16),
            pltpu.VMEM((classes, held), jnp.bfloat16),
            pltpu.VMEM(blocks, jnp.bfloat16),
            pltpu.SemaphoreType.DMA((plane * count // STEP,)),
            pltpu.SemaphoreType.DMA((plane * count // STEP,)),
        ],
        compiler_params=pltpu.CompilerParams(vmem_limit_bytes=48 * 2**20),
        cost_estimate=pl.CostEstimate(
            flops=2 * plane * count * held * (features + classes),
            bytes_accessed=9 * 2**20,
            transcendentals=plane * count * held,
        ),
        name="classify",
    )(*parts, panel)
    parts = exchange(parts, PLANE)
    return pl.pallas_call(
        combine,
        out_shape=jax.ShapeDtypeStruct((count, classes), jnp.bfloat16),
        compiler_params=pltpu.CompilerParams(vmem_limit_bytes=20 * 2**20),
        cost_estimate=pl.CostEstimate(
            flops=2 * plane * count * classes, bytes_accessed=3 * 2**20, transcendentals=0
        ),
        name="combine",
    )(parts)


def solution(mesh):
    chips = Mesh(mesh.devices.reshape(SIZES), AXES)
    placed = P(AXES, None)
    return jax.shard_map(
        shards, mesh=chips, in_specs=(placed, placed, placed), out_specs=placed, check_vma=False
    )
```

time: 114 us -> 111 us (0.974)
  local copies, waits for them, and re-layouts: 5.43 us -> 3.02 us
  Pallas kernels: 11.1 us -> 9.71 us
    unnamed x13 -> x5, local copies, waits for them, and re-layouts: 2.51 us -> 0.03 us
    pallas_call x1, Pallas kernels: 9.89 us -> 8.52 us  [shards(): pl.pallas_call(functools.partial(classify, sharpness), in_specs=[inside]...]
where the time goes in v2:
time: 111 us; the launch traced here: 110 us
  blocking collectives  70.5 us (64%)
  starting transfers between devices  25.3 us (23%)
  Pallas kernels  9.71 us (9%)
  local copies, waits for them, and re-layouts  3.02 us (3%)
  waiting for transfers between devices  1.7 us (2%)
    all_to_all x1, blocking collectives, exchange(): return lax.all_to_all(value, axes, 0, 0, tiled=True)  35.6 us
    all_gather x1, blocking collectives, shards(): same = lax.all_gather(rows, 'z_hi', axis=0, tiled=True)  35 us
    ppermute x4, starting transfers between devices, shifted(): lax.ppermute(value, axes, [(i, (i + by) % devices) for i in range(devices)])  17.6 us
    pallas_call x1, Pallas kernels, shards(): pl.pallas_call(functools.partial(classify, sharpness), in_specs=[inside]...  8.52 us
    all_to_all x1, starting transfers between devices, exchange(): return lax.all_to_all(value, axes, 0, 0, tiled=True)  7.76 us
    broadcast_in_dim x1, local copies, waits for them, and re-layouts, copies(): jnp.broadcast_to(value[None], (count, rows, width))  2.93 us
  transfers between devices with their start and end apart: 5, of which 1 were waited for; matrix products, arithmetic and copies ran while one was open for 0% of the time, Pallas kernels for 0%

profile of v2, /device:TPU:1, one launch (start us, length us, event | category | flops | bytes accessed | tf_op | source)
XLA Modules:
  0.0 110.5 jit_solution(3511159350768888279)
XLA Ops:
  0.0 2.9 %broadcast_in_dim.2 = bf16[16,128,768]{2,1,0:T(8,128)(2,1)} broadcast(bf16[128,768]{1,0:T(8,128)(2,1)} %param.3), dimensions={1,2} | broadcast | bytes 3342336 | tf_op jit(solution)/shard_map/broadcast_in_dim | solution.py:22
  2.9 0.0 copy-start
  2.9 0.0 copy-start.1
  2.9 7.8 %all-to-all-start = ((bf16[16,128,768]{2,1,0:T(8,128)(2,1)}), bf16[16,128,768]{2,1,0:T(8,128)(2,1)}, u32[]{:S(2)}, u32[]{:S(2)}) async-start(bf16[16,128,768]{2,1,0:T(8,128)(2,1)} %broadcast_in_dim.2), calls=%async_computation | async-start | bytes 6291456 | tf_op jit(solution)/shard_map/all_to_all | solution.py:26
  10.7 0.0 copy-done
  10.7 0.0 copy-done.1
  10.7 35.0 %all_gather.3.refs_0_ = bf16[256,1280]{1,0:T(8,128)(2,1)S(1)} all-gather(bf16[32,1280]{1,0:T(8,128)(2,1)S(1)} %pad_maximum_fusion), channel_id=1, replica_groups=mesh['x_lo'=2,'z_hi'=8,'z_lo'=2,'core'=2,'y'=4,'x_hi'=2] {'z_hi'}, dimensions={0}, use_global_device_ids=true | all-gather | bytes 737280 | tf_op jit(solution)/shard_map/all_gather | solution.py:136
  45.7 2.0 %collective-permute-start.1 = (bf16[128,1280]{1,0:T(8,128)(2,1)S(1)}, bf16[128,1280]{1,0:T(8,128)(2,1)S(1)}, u32[]{:S(2)}, u32[]{:S(2)}) collective-permute-start(bf16[128,1280]{1,0:T(8,128)(2,1)S(1)} %get-tuple-element.6), channel_id=1, source_target_pairs={{0,16},{16,32},{32,48},{48,64},{64,80},{80,96},{96,112},{112,128},... | collective-permute-start | bytes 983048 | tf_op jit(solution)/shard_map/ppermute | solution.py:31
  47.7 4.5 %collective-permute-start.2 = (bf16[128,1280]{1,0:T(8,128)(2,1)S(1)}, bf16[128,1280]{1,0:T(8,128)(2,1)S(1)}, u32[]{:S(2)}, u32[]{:S(2)}) collective-permute-start(bf16[128,1280]{1,0:T(8,128)(2,1)S(1)} %get-tuple-element.5), channel_id=1, source_target_pairs={{0,240},{16,0},{32,16},{48,32},{64,48},{80,64},{96,80},{112,96},{1... | collective-permute-start | bytes 983048 | tf_op jit(solution)/shard_map/ppermute | solution.py:31
  52.2 6.6 %collective-permute-start = (bf16[256,1280]{1,0:T(8,128)(2,1)S(1)}, bf16[256,1280]{1,0:T(8,128)(2,1)S(1)}, u32[]{:S(2)}, u32[]{:S(2)}) collective-permute-start(bf16[256,1280]{1,0:T(8,128)(2,1)S(1)} %all_gather.3.refs_0_), channel_id=1, source_target_pairs={{0,8},{8,0},{1,9},{9,1},{2,10},{10,2},{3,11},{11,3},{4,12},{12,4},... | collective-permute-start | bytes 1966088 | tf_op jit(solution)/shard_map/ppermute | solution.py:31
  58.8 0.0 collective-permute-done.1
  58.9 0.0 collective-permute-done.2
  58.9 4.5 %collective-permute-start.3 = (bf16[256,1280]{1,0:T(8,128)(2,1)S(1)}, bf16[256,1280]{1,0:T(8,128)(2,1)S(1)}, u32[]{:S(2)}, u32[]{:S(2)}) collective-permute-start(bf16[256,1280]{1,0:T(8,128)(2,1)S(1)} %constant_dynamic-update-slice_fusion.refs_2_), channel_id=1, source_target_pairs={{0,8},{8,0},{1,9},{9,1},{2,10},{10,2},{3,11},{11,3},{4,12},{12,4},... | collective-permute-start | bytes 1966088 | tf_op jit(solution)/shard_map/ppermute | solution.py:31
  63.4 0.0 collective-permute-done.refs_1_
  63.5 1.7 %collective-permute-done.3.refs_3_ = bf16[256,1280]{1,0:T(8,128)(2,1)S(1)} collective-permute-done((bf16[256,1280]{1,0:T(8,128)(2,1)S(1)}, bf16[256,1280]{1,0:T(8,128)(2,1)S(1)}, u32[]{:S(2)}, u32[]{:S(2)}) %collective-permute-start.3) | collective-permute-done | bytes 655392 | tf_op jit(solution)/shard_map/ppermute | solution.py:31
  65.1 0.0 all-to-all-done
  65.2 8.5 %classify.1 = bf16[16,528,128]{2,1,0:T(8,128)(2,1)S(1)} custom-call(bf16[256,1280]{1,0:T(8,128)(2,1)S(1)} %all_gather.3.refs_0_, bf16[256,1280]{1,0:T(8,128)(2,1)S(1)} %collective-permute-done.refs_1_, bf16[256,1280]{1,0:T(8,128)(2,1)S(1)} %constant_dynamic-update-slice_fusion.refs_2_, bf16[256,1280]{1,0:T(8,128)(2,1)S(1)} %collective-permute-done.3.refs_3_, ...), custom_call_target="tpu_custom_call" | custom-call | flops 5368709120 | bytes 9437184 | tf_op jit(solution)/shard_map/classify/pallas_call | solution.py:143
  73.7 35.6 %all_to_all.13.parts_ref = bf16[16,528,128]{2,1,0:T(8,128)(2,1)S(1)} all-to-all(bf16[16,528,128]{2,1,0:T(8,128)(2,1)S(1)} %classify.1), channel_id=1, replica_groups=mesh['x_lo'=2,'z_hi'=8,'z_lo'=2,'core'=2,'y'=4,'x_hi'=2] {'x_lo','y','x_..., dimensions={0} | all-to-all | bytes 4325376 | tf_op jit(solution)/shard_map/all_to_all | solution.py:26
  109.3 1.2 %combine.1 = bf16[128,512]{1,0:T(8,128)(2,1)} custom-call(bf16[16,528,128]{2,1,0:T(8,128)(2,1)S(1)} %all_to_all.13.parts_ref), custom_call_target="tpu_custom_call" | custom-call | flops 2097152 | bytes 3145728 | tf_op jit(solution)/shard_map/combine/pallas_call | solution.py:164
  (4 shorter events, 0.1 us)
Async XLA Ops:
  2.9 7.8 %copy-start = (bf16[32,768]{1,0:T(8,128)(2,1)S(1)}, bf16[32,768]{1,0:T(8,128)(2,1)}, u32[]{:S(2)}) copy-start(bf16[32,768]{1,0:T(8,128)(2,1)} %param.4) | copy-start | bytes 147460
  2.9 7.8 %copy-start.1 = (bf16[32,512]{1,0:T(8,128)(2,1)S(1)}, bf16[32,512]{1,0:T(8,128)(2,1)}, u32[]{:S(2)}) copy-start(bf16[32,512]{1,0:T(8,128)(2,1)} %param.5) | copy-start | bytes 98308
  2.9 62.2 %all-to-all-start = ((bf16[16,128,768]{2,1,0:T(8,128)(2,1)}), bf16[16,128,768]{2,1,0:T(8,128)(2,1)}, u32[]{:S(2)}, u32[]{:S(2)}) async-start(bf16[16,128,768]{2,1,0:T(8,128)(2,1)} %broadcast_in_dim.2), calls=%async_computation | async-start | bytes 6291456 | tf_op jit(solution)/shard_map/all_to_all | solution.py:26
  45.7 13.1 %collective-permute-start.1 = (bf16[128,1280]{1,0:T(8,128)(2,1)S(1)}, bf16[128,1280]{1,0:T(8,128)(2,1)S(1)}, u32[]{:S(2)}, u32[]{:S(2)}) collective-permute-start(bf16[128,1280]{1,0:T(8,128)(2,1)S(1)} %get-tuple-element.6), channel_id=1, source_target_pairs={{0,16},{16,32},{32,48},{48,64},{64,80},{80,96},{96,112},{112,128},... | collective-permute-start | bytes 983048 | tf_op jit(solution)/shard_map/ppermute | solution.py:31
  47.7 11.2 %collective-permute-start.2 = (bf16[128,1280]{1,0:T(8,128)(2,1)S(1)}, bf16[128,1280]{1,0:T(8,128)(2,1)S(1)}, u32[]{:S(2)}, u32[]{:S(2)}) collective-permute-start(bf16[128,1280]{1,0:T(8,128)(2,1)S(1)} %get-tuple-element.5), channel_id=1, source_target_pairs={{0,240},{16,0},{32,16},{48,32},{64,48},{80,64},{96,80},{112,96},{1... | collective-permute-start | bytes 983048 | tf_op jit(solution)/shard_map/ppermute | solution.py:31
  52.2 11.2 %collective-permute-start = (bf16[256,1280]{1,0:T(8,128)(2,1)S(1)}, bf16[256,1280]{1,0:T(8,128)(2,1)S(1)}, u32[]{:S(2)}, u32[]{:S(2)}) collective-permute-start(bf16[256,1280]{1,0:T(8,128)(2,1)S(1)} %all_gather.3.refs_0_), channel_id=1, source_target_pairs={{0,8},{8,0},{1,9},{9,1},{2,10},{10,2},{3,11},{11,3},{4,12},{12,4},... | collective-permute-start | bytes 1966088 | tf_op jit(solution)/shard_map/ppermute | solution.py:31
  58.9 6.2 %collective-permute-start.3 = (bf16[256,1280]{1,0:T(8,128)(2,1)S(1)}, bf16[256,1280]{1,0:T(8,128)(2,1)S(1)}, u32[]{:S(2)}, u32[]{:S(2)}) collective-permute-start(bf16[256,1280]{1,0:T(8,128)(2,1)S(1)} %constant_dynamic-update-slice_fusion.refs_2_), channel_id=1, source_target_pairs={{0,8},{8,0},{1,9},{9,1},{2,10},{10,2},{3,11},{11,3},{4,12},{12,4},... | collective-permute-start | bytes 1966088 | tf_op jit(solution)/shard_map/ppermute | solution.py:31

commit v3 on v2

v3 whole, which is shorter than its diff:
```python
import functools
import math

import jax
import jax.numpy as jnp
from jax import lax
from jax.experimental import pallas as pl
from jax.experimental.pallas import tpu as pltpu
from jax.sharding import Mesh
from jax.sharding import PartitionSpec as P

AXES = ("x_lo", "z_hi", "z_lo", "core", "y", "x_hi")
SIZES = (2, 8, 2, 2, 4, 2)
ZX = ("x_lo", "z_hi", "z_lo", "x_hi")
GROUP = ("y", "x_hi")
EXTRA = 16
STEP = 512


def copies(value, count):
    rows, width = value.shape
    return jnp.broadcast_to(value[None], (count, rows, width)).reshape(count * rows, width)


def exchange(value, axes):
    return lax.all_to_all(value, axes, 0, 0, tiled=True)


def moved(value, along_x, along_z):
    columns = lax.axis_size("x_lo") * lax.axis_size("x_hi")
    height = lax.axis_size("z_hi") * lax.axis_size("z_lo")

    def place(x, z):
        x, z = x % columns, z % height
        return ((x % 2) * height + z) * 2 + x // 2

    return lax.ppermute(
        value,
        ZX,
        [
            (place(x, z), place(x + along_x, z + along_z))
            for x in range(columns)
            for z in range(height)
        ],
    )


def swapped(value):
    return lax.ppermute(value, "core", [(0, 1), (1, 0)])


def classify(sharpness, pieces, resumes, ends, *refs):
    refs = list(refs)
    row_refs, refs = refs[:pieces], refs[pieces:]
    queries_ref = refs.pop(0)
    if resumes:
        past_ref, past_stats_ref = refs.pop(0), refs.pop(0)
    if ends:
        parts_ref, labels_ref, out_ref, departures = refs
    else:
        weighted_ref, stats_ref, labels_ref = refs
    features = queries_ref.shape[1]
    panels = queries_ref.shape[0] // STEP
    bounds = [0]
    for ref in row_refs:
        bounds.append(bounds[-1] + ref.shape[0])
    for index, ref in enumerate(row_refs):
        labels_ref[:, bounds[index] : bounds[index + 1]] = ref[:, features:].T

    def products(panel):
        return [
            lax.dot_general(
                ref[:, :features],
                queries_ref[panel * STEP : (panel + 1) * STEP, :],
                (((1,), (1,)), ((), ())),
                preferred_element_type=jnp.float32,
            )
            for ref in row_refs
        ]

    rate = sharpness * math.log2(math.e)
    later = products(0)
    sends = []
    for panel in range(panels):
        now, later = later, products(panel + 1) if panel + 1 < panels else None
        columns = slice(panel * STEP, (panel + 1) * STEP)
        top = functools.reduce(jnp.maximum, [jnp.max(part, axis=0, keepdims=True) for part in now])
        if resumes:
            past_top = past_stats_ref[0:1, columns]
            top = jnp.maximum(top, past_top)
            fade = jnp.exp2((past_top - top) * rate)
        weights = [jnp.exp2((part - top) * rate) for part in now]
        total = sum(jnp.sum(part, axis=0, keepdims=True) for part in weights)
        weighted = sum(
            jnp.dot(
                labels_ref[:, bounds[index] : bounds[index + 1]],
                part.astype(jnp.bfloat16),
                preferred_element_type=jnp.float32,
            )
            for index, part in enumerate(weights)
        )
        if resumes:
            total = total + fade * past_stats_ref[1:2, columns]
            weighted = weighted + fade * past_ref[:, columns]
        if not ends:
            weighted_ref[:, columns] = weighted
            stats_ref[0:1, columns] = top
            stats_ref[1:2, columns] = total
            continue
        mean = (weighted * (1.0 / total)).astype(jnp.bfloat16)
        level = top * sharpness + jnp.log(total)
        first = level.astype(jnp.bfloat16).astype(jnp.float32)
        second = (level - first).astype(jnp.bfloat16).astype(jnp.float32)
        third = level - first - second
        row = lax.broadcasted_iota(jnp.int32, (EXTRA, STEP), 0)
        levels = jnp.where(
            row == 0, first, jnp.where(row == 1, second, jnp.where(row == 2, third, 0.0))
        ).astype(jnp.bfloat16)
        blocks, classes, wide = out_ref.shape
        classes -= EXTRA
        per_panel = blocks // panels
        for index in range(per_panel):
            block = panel * per_panel + index
            out_ref[block, :classes, :] = mean[:, index * wide : (index + 1) * wide]
            out_ref[block, classes:, :] = levels[:, index * wide : (index + 1) * wide]
        done = slice(panel * per_panel, (panel + 1) * per_panel)
        send = pltpu.make_async_copy(out_ref.at[done], parts_ref.at[done], departures.at[panel])
        send.start()
        sends.append(send)
    for send in sends:
        send.wait()


def combine(parts_ref, out_ref):
    sources = parts_ref.shape[0]
    classes = parts_ref.shape[1] - EXTRA
    levels = [
        jnp.sum(parts_ref[source, classes:, :].astype(jnp.float32), axis=0, keepdims=True)
        for source in range(sources)
    ]
    top = functools.reduce(jnp.maximum, levels)
    shares = [jnp.exp(level - top) for level in levels]
    scale = 1.0 / sum(shares)
    shares = [share * scale for share in shares]
    for at in range(0, classes, 128):
        mean = sum(
            shares[source] * parts_ref[source, at : at + 128, :].astype(jnp.float32)
            for source in range(sources)
        )
        out_ref[:, at : at + 128] = mean.T.astype(out_ref.dtype)


def shards(queries, keys, labels):
    count, features = queries.shape
    classes = labels.shape[1]
    group = lax.axis_size(GROUP)
    anywhere = pl.BlockSpec(memory_space=pltpu.HBM)
    inside = pl.BlockSpec(memory_space=pltpu.VMEM)
    sharpness = 2.5 / math.sqrt(features)

    panel = exchange(copies(queries, group), GROUP)

    rows = jnp.concatenate([keys, labels], axis=1)
    same = lax.all_gather(rows, "z_hi", axis=0, tiled=True)
    same, panel = lax.optimization_barrier((same, panel))
    others = [moved(same, 1, -1), moved(same, 0, 1), moved(same, -1, 0)]

    blocks = (group, classes + EXTRA, count)
    asked = group * count

    def taken(row_parts, running, ends):
        held = sum(part.shape[0] for part in row_parts)
        operands = [*row_parts, panel, *running]
        scratch = [pltpu.VMEM((classes, held), jnp.bfloat16)]
        if ends:
            out_specs = anywhere
            out_shape = jax.ShapeDtypeStruct(blocks, jnp.bfloat16)
            scratch += [
                pltpu.VMEM(blocks, jnp.bfloat16),
                pltpu.SemaphoreType.DMA((asked // STEP,)),
            ]
        else:
            out_specs = [inside, inside]
            out_shape = [
                jax.ShapeDtypeStruct((classes, asked), jnp.float32),
                jax.ShapeDtypeStruct((8, asked), jnp.float32),
            ]
        return pl.pallas_call(
            functools.partial(classify, sharpness, len(row_parts), bool(running), ends),
            in_specs=[inside] * len(operands),
            out_specs=out_specs,
            out_shape=out_shape,
            scratch_shapes=scratch,
            compiler_params=pltpu.CompilerParams(vmem_limit_bytes=40 * 2**20),
            cost_estimate=pl.CostEstimate(
                flops=2 * asked * held * (features + classes),
                bytes_accessed=4 * 2**20,
                transcendentals=asked * held,
            ),
            name="classify",
        )(*operands)

    others = jnp.concatenate(others, axis=0)
    near = jnp.concatenate([same, others], axis=0)
    running = taken([near], (), False)
    parts = taken([swapped(near)], running, True)
    parts = exchange(parts, GROUP)
    return pl.pallas_call(
        combine,
        out_shape=jax.ShapeDtypeStruct((count, classes), jnp.bfloat16),
        compiler_params=pltpu.CompilerParams(vmem_limit_bytes=20 * 2**20),
        cost_estimate=pl.CostEstimate(
            flops=2 * group * count * classes, bytes_accessed=3 * 2**20, transcendentals=0
        ),
        name="combine",
    )(parts)


def solution(mesh):
    chips = Mesh(mesh.devices.reshape(SIZES), AXES)
    placed = P(AXES, None)
    return jax.shard_map(
        shards, mesh=chips, in_specs=(placed, placed, placed), out_specs=placed, check_vma=False
    )
```

time: 111 us -> 104 us (0.937)
  blocking collectives: 70.5 us -> 57.5 us
  waiting for transfers between devices: 1.7 us -> 9.74 us
  Pallas kernels: 9.71 us -> 8 us
    all_to_all x1, blocking collectives: 35.6 us -> 23.4 us  [exchange(): return lax.all_to_all(value, axes, 0, 0, tiled=True)]
    ppermute x4, waiting for transfers between devices: 1.7 us -> 9.74 us  [the longest x3 8.58 us: moved(): lax.ppermute(value, ZX, [(place(x, z), place(x + along_x, z + along_z)) f...]
    pallas_call x1 -> x2, Pallas kernels: 8.52 us -> 7.03 us  [taken(): pl.pallas_call(functools.partial(classify, sharpness, len(row_parts), boo...]
  transfers between devices with their start and end apart: 5 -> 5, of which waited for: 1 -> 4; matrix products, arithmetic and copies ran while one was open for 0% -> 0% of each run, Pallas kernels for 0% -> 3%
where the time goes in v3:
time: 104 us; the launch traced here: 103 us
  blocking collectives  57.5 us (55%)
  starting transfers between devices  25.8 us (25%)
  waiting for transfers between devices  9.74 us (9%)
  Pallas kernels  8 us (8%)
  local copies, waits for them, and re-layouts  2.37 us (2%)
    all_gather x1, blocking collectives, shards(): same = lax.all_gather(rows, 'z_hi', axis=0, tiled=True)  34.1 us
    all_to_all x1, blocking collectives, exchange(): return lax.all_to_all(value, axes, 0, 0, tiled=True)  23.4 us
    ppermute x3, starting transfers between devices, moved(): lax.ppermute(value, ZX, [(place(x, z), place(x + along_x, z + along_z)) f...  9.93 us
    ppermute x3, waiting for transfers between devices, moved(): lax.ppermute(value, ZX, [(place(x, z), place(x + along_x, z + along_z)) f...  8.58 us
    ppermute x1, starting transfers between devices, swapped(): return lax.ppermute(value, 'core', [(0, 1), (1, 0)])  8.39 us
    all_to_all x1, starting transfers between devices, exchange(): return lax.all_to_all(value, axes, 0, 0, tiled=True)  7.48 us
    pallas_call x2, Pallas kernels, taken(): pl.pallas_call(functools.partial(classify, sharpness, len(row_parts), boo...  7.03 us
    broadcast_in_dim x1, local copies, waits for them, and re-layouts, copies(): jnp.broadcast_to(value[None], (count, rows, width))  2.19 us
  transfers between devices with their start and end apart: 5, of which 4 were waited for; matrix products, arithmetic and copies ran while one was open for 0% of the time, Pallas kernels for 3%

profile of v3, /device:TPU:1, one launch (start us, length us, event | category | flops | bytes accessed | tf_op | source)
XLA Modules:
  0.0 103.5 jit_solution(9776352505156138417)
XLA Ops:
  0.0 0.0 copy-start.1
  0.0 0.0 copy-start
  0.0 2.2 %broadcast_in_dim.2 = bf16[8,128,768]{2,1,0:T(8,128)(2,1)} broadcast(bf16[128,768]{1,0:T(8,128)(2,1)} %param.3), dimensions={1,2} | broadcast | bytes 1769472 | tf_op jit(solution)/shard_map/broadcast_in_dim | solution.py:22
  2.2 7.5 %all-to-all-start = ((bf16[8,128,768]{2,1,0:T(8,128)(2,1)}), bf16[8,128,768]{2,1,0:T(8,128)(2,1)S(1)}, u32[]{:S(2)}, u32[]{:S(2)}) async-start(bf16[8,128,768]{2,1,0:T(8,128)(2,1)} %broadcast_in_dim.2), calls=%async_computation | async-start | bytes 3145728 | tf_op jit(solution)/shard_map/all_to_all | solution.py:26
  9.7 0.0 copy-done.1
  9.7 0.0 copy-done
  9.7 34.1 %all_gather.3 = bf16[256,1280]{1,0:T(8,128)(2,1)S(1)} all-gather(bf16[32,1280]{1,0:T(8,128)(2,1)S(1)} %pad_maximum_fusion), channel_id=1, replica_groups=mesh['x_lo'=2,'z_hi'=8,'z_lo'=2,'core'=2,'y'=4,'x_hi'=2] {'z_hi'}, dimensions={0}, use_global_device_ids=true | all-gather | bytes 737280 | tf_op jit(solution)/shard_map/all_gather | solution.py:164
  43.8 0.0 all-to-all-done
  43.8 3.4 %collective-permute-start = (bf16[256,1280]{1,0:T(8,128)(2,1)S(1)}, bf16[256,1280]{1,0:T(8,128)(2,1)S(1)}, u32[]{:S(2)}, u32[]{:S(2)}) collective-permute-start(bf16[256,1280]{1,0:T(8,128)(2,1)S(1)} %all_gather.3), channel_id=1, source_target_pairs={{0,496},{16,256},{32,272},{48,288},{64,304},{80,320},{96,336},{112... | collective-permute-start | bytes 1966088 | tf_op jit(solution)/shard_map/ppermute | solution.py:37
  47.2 1.9 %collective-permute-start.1 = (bf16[256,1280]{1,0:T(8,128)(2,1)S(1)}, bf16[256,1280]{1,0:T(8,128)(2,1)S(1)}, u32[]{:S(2)}, u32[]{:S(2)}) collective-permute-start(bf16[256,1280]{1,0:T(8,128)(2,1)S(1)} %all_gather.3), channel_id=1, source_target_pairs={{0,16},{16,32},{32,48},{48,64},{64,80},{80,96},{96,112},{112,128},... | collective-permute-start | bytes 1966088 | tf_op jit(solution)/shard_map/ppermute | solution.py:37
  49.1 4.6 %collective-permute-start.2 = (bf16[256,1280]{1,0:T(8,128)(2,1)S(1)}, bf16[256,1280]{1,0:T(8,128)(2,1)S(1)}, u32[]{:S(2)}, u32[]{:S(2)}) collective-permute-start(bf16[256,1280]{1,0:T(8,128)(2,1)S(1)} %all_gather.3), channel_id=1, source_target_pairs={{0,257},{16,273},{32,289},{48,305},{64,321},{80,337},{96,353},{112... | collective-permute-start | bytes 1966088 | tf_op jit(solution)/shard_map/ppermute | solution.py:37
  53.8 5.2 %collective-permute-done = bf16[256,1280]{1,0:T(8,128)(2,1)S(1)} collective-permute-done((bf16[256,1280]{1,0:T(8,128)(2,1)S(1)}, bf16[256,1280]{1,0:T(8,128)(2,1)S(1)}, u32[]{:S(2)}, u32[]{:S(2)}) %collective-permute-start) | collective-permute-done | bytes 655392 | tf_op jit(solution)/shard_map/ppermute | solution.py:37
  59.1 2.1 %collective-permute-done.1 = bf16[256,1280]{1,0:T(8,128)(2,1)S(1)} collective-permute-done((bf16[256,1280]{1,0:T(8,128)(2,1)S(1)}, bf16[256,1280]{1,0:T(8,128)(2,1)S(1)}, u32[]{:S(2)}, u32[]{:S(2)}) %collective-permute-start.1) | collective-permute-done | bytes 655392 | tf_op jit(solution)/shard_map/ppermute | solution.py:37
  61.3 1.2 %collective-permute-done.2 = bf16[256,1280]{1,0:T(8,128)(2,1)S(1)} collective-permute-done((bf16[256,1280]{1,0:T(8,128)(2,1)S(1)}, bf16[256,1280]{1,0:T(8,128)(2,1)S(1)}, u32[]{:S(2)}, u32[]{:S(2)}) %collective-permute-start.2) | collective-permute-done | bytes 655392 | tf_op jit(solution)/shard_map/ppermute | solution.py:37
  62.5 8.4 %collective-permute-start.3 = (bf16[1024,1280]{1,0:T(8,128)(2,1)S(1)}, bf16[1024,1280]{1,0:T(8,128)(2,1)S(1)}, u32[]{:S(2)}, u32[]{:S(2)}) collective-permute-start(bf16[1024,1280]{1,0:T(8,128)(2,1)S(1)} %constant_dynamic-update-slice_fusion.refs_0_), channel_id=1, source_target_pairs={{0,8},{8,0},{1,9},{9,1},{2,10},{10,2},{3,11},{11,3},{4,12},{12,4},... | collective-permute-start | bytes 7864328 | tf_op jit(solution)/shard_map/ppermute | solution.py:49
  70.9 3.4 %classify.2 = (f32[512,1024]{1,0:T(8,128)S(1)}, f32[8,1024]{1,0:T(8,128)S(1)}) custom-call(bf16[1024,1280]{1,0:T(8,128)(2,1)S(1)} %constant_dynamic-update-slice_fusion.refs_0_, bf16[1024,768]{1,0:T(8,128)(2,1)S(1)} %bitcast.1), custom_call_target="tpu_custom_call" | custom-call | flops 2684354560 | bytes 4194304 | tf_op jit(solution)/shard_map/classify/pallas_call | solution.py:188
  74.3 1.2 %collective-permute-done.3.refs_0_ = bf16[1024,1280]{1,0:T(8,128)(2,1)S(1)} collective-permute-done((bf16[1024,1280]{1,0:T(8,128)(2,1)S(1)}, bf16[1024,1280]{1,0:T(8,128)(2,1)S(1)}, u32[]{:S(2)}, u32[]{:S(2)}) %collective-permute-start.3) | collective-permute-done | bytes 2621472 | tf_op jit(solution)/shard_map/ppermute | solution.py:49
  75.4 3.7 %classify.3 = bf16[8,528,128]{2,1,0:T(8,128)(2,1)S(1)} custom-call(bf16[1024,1280]{1,0:T(8,128)(2,1)S(1)} %collective-permute-done.3.refs_0_, bf16[1024,768]{1,0:T(8,128)(2,1)S(1)} %bitcast.2, f32[512,1024]{1,0:T(8,128)S(1)} %get-tuple-element.11.refs_2_, f32[8,1024]{1,0:T(8,128)S(1)} %get-tuple-element.12.refs_3_), custom_call_target="tpu_custom_call" | custom-call | flops 2684354560 | bytes 4194304 | tf_op jit(solution)/shard_map/classify/pallas_call | solution.py:188
  79.1 23.4 %all_to_all.14.parts_ref = bf16[8,528,128]{2,1,0:T(8,128)(2,1)S(1)} all-to-all(bf16[8,528,128]{2,1,0:T(8,128)(2,1)S(1)} %classify.3), channel_id=1, replica_groups=mesh['x_lo'=2,'z_hi'=8,'z_lo'=2,'core'=2,'y'=4,'x_hi'=2] {'y','x_hi'}, dimensions={0} | all-to-all | bytes 2162688 | tf_op jit(solution)/shard_map/all_to_all | solution.py:26
  102.5 1.0 combine.1
  (5 shorter events, 0.2 us)
Async XLA Ops:
  0.0 9.7 %copy-start.1 = (bf16[32,512]{1,0:T(8,128)(2,1)S(1)}, bf16[32,512]{1,0:T(8,128)(2,1)}, u32[]{:S(2)}) copy-start(bf16[32,512]{1,0:T(8,128)(2,1)} %param.5) | copy-start | bytes 98308
  0.0 9.7 %copy-start = (bf16[32,768]{1,0:T(8,128)(2,1)S(1)}, bf16[32,768]{1,0:T(8,128)(2,1)}, u32[]{:S(2)}) copy-start(bf16[32,768]{1,0:T(8,128)(2,1)} %param.4) | copy-start | bytes 147460
  2.2 41.6 %all-to-all-start = ((bf16[8,128,768]{2,1,0:T(8,128)(2,1)}), bf16[8,128,768]{2,1,0:T(8,128)(2,1)S(1)}, u32[]{:S(2)}, u32[]{:S(2)}) async-start(bf16[8,128,768]{2,1,0:T(8,128)(2,1)} %broadcast_in_dim.2), calls=%async_computation | async-start | bytes 3145728 | tf_op jit(solution)/shard_map/all_to_all | solution.py:26
  43.8 15.2 %collective-permute-start = (bf16[256,1280]{1,0:T(8,128)(2,1)S(1)}, bf16[256,1280]{1,0:T(8,128)(2,1)S(1)}, u32[]{:S(2)}, u32[]{:S(2)}) collective-permute-start(bf16[256,1280]{1,0:T(8,128)(2,1)S(1)} %all_gather.3), channel_id=1, source_target_pairs={{0,496},{16,256},{32,272},{48,288},{64,304},{80,320},{96,336},{112... | collective-permute-start | bytes 1966088 | tf_op jit(solution)/shard_map/ppermute | solution.py:37
  47.2 14.0 %collective-permute-start.1 = (bf16[256,1280]{1,0:T(8,128)(2,1)S(1)}, bf16[256,1280]{1,0:T(8,128)(2,1)S(1)}, u32[]{:S(2)}, u32[]{:S(2)}) collective-permute-start(bf16[256,1280]{1,0:T(8,128)(2,1)S(1)} %all_gather.3), channel_id=1, source_target_pairs={{0,16},{16,32},{32,48},{48,64},{64,80},{80,96},{96,112},{112,128},... | collective-permute-start | bytes 1966088 | tf_op jit(solution)/shard_map/ppermute | solution.py:37
  49.1 13.3 %collective-permute-start.2 = (bf16[256,1280]{1,0:T(8,128)(2,1)S(1)}, bf16[256,1280]{1,0:T(8,128)(2,1)S(1)}, u32[]{:S(2)}, u32[]{:S(2)}) collective-permute-start(bf16[256,1280]{1,0:T(8,128)(2,1)S(1)} %all_gather.3), channel_id=1, source_target_pairs={{0,257},{16,273},{32,289},{48,305},{64,321},{80,337},{96,353},{112... | collective-permute-start | bytes 1966088 | tf_op jit(solution)/shard_map/ppermute | solution.py:37
  62.5 12.9 %collective-permute-start.3 = (bf16[1024,1280]{1,0:T(8,128)(2,1)S(1)}, bf16[1024,1280]{1,0:T(8,128)(2,1)S(1)}, u32[]{:S(2)}, u32[]{:S(2)}) collective-permute-start(bf16[1024,1280]{1,0:T(8,128)(2,1)S(1)} %constant_dynamic-update-slice_fusion.refs_0_), channel_id=1, source_target_pairs={{0,8},{8,0},{1,9},{9,1},{2,10},{10,2},{3,11},{11,3},{4,12},{12,4},... | collective-permute-start | bytes 7864328 | tf_op jit(solution)/shard_map/ppermute | solution.py:49

commit v4 on v3

--- a/solution.py
+++ b/solution.py
@@ -56,7 +56,7 @@
     if resumes:
         past_ref, past_stats_ref = refs.pop(0), refs.pop(0)
     if ends:
-        parts_ref, labels_ref, out_ref, departures = refs
+        out_ref, labels_ref = refs
     else:
         weighted_ref, stats_ref, labels_ref = refs
     features = queries_ref.shape[1]
@@ -80,7 +80,6 @@
 
     rate = sharpness * math.log2(math.e)
     later = products(0)
-    sends = []
     for panel in range(panels):
         now, later = later, products(panel + 1) if panel + 1 < panels else None
         columns = slice(panel * STEP, (panel + 1) * STEP)
@@ -123,12 +122,6 @@
             block = panel * per_panel + index
             out_ref[block, :classes, :] = mean[:, index * wide : (index + 1) * wide]
             out_ref[block, classes:, :] = levels[:, index * wide : (index + 1) * wide]
-        done = slice(panel * per_panel, (panel + 1) * per_panel)
-        send = pltpu.make_async_copy(out_ref.at[done], parts_ref.at[done], departures.at[panel])
-        send.start()
-        sends.append(send)
-    for send in sends:
-        send.wait()
 
 
 def combine(parts_ref, out_ref):
@@ -154,7 +147,6 @@
     count, features = queries.shape
     classes = labels.shape[1]
     group = lax.axis_size(GROUP)
-    anywhere = pl.BlockSpec(memory_space=pltpu.HBM)
     inside = pl.BlockSpec(memory_space=pltpu.VMEM)
     sharpness = 2.5 / math.sqrt(features)
 
@@ -163,7 +155,7 @@
     rows = jnp.concatenate([keys, labels], axis=1)
     same = lax.all_gather(rows, "z_hi", axis=0, tiled=True)
     same, panel = lax.optimization_barrier((same, panel))
-    others = [moved(same, 1, -1), moved(same, 0, 1), moved(same, -1, 0)]
+    others = [moved(same, -1, 0), moved(same, 0, 1), moved(same, 1, -1)]
 
     blocks = (group, classes + EXTRA, count)
     asked = group * count
@@ -173,12 +165,8 @@
         operands = [*row_parts, panel, *running]
         scratch = [pltpu.VMEM((classes, held), jnp.bfloat16)]
         if ends:
-            out_specs = anywhere
+            out_specs = inside
             out_shape = jax.ShapeDtypeStruct(blocks, jnp.bfloat16)
-            scratch += [
-                pltpu.VMEM(blocks, jnp.bfloat16),
-                pltpu.SemaphoreType.DMA((asked // STEP,)),
-            ]
         else:
             out_specs = [inside, inside]
             out_shape = [
@@ -200,10 +188,13 @@
             name="classify",
         )(*operands)
 
+    running = taken([same], (), False)
+    same_late, running = lax.optimization_barrier((same, running))
+    far_same = swapped(same_late)
+    others, far_same = lax.optimization_barrier((others, far_same))
     others = jnp.concatenate(others, axis=0)
-    near = jnp.concatenate([same, others], axis=0)
-    running = taken([near], (), False)
-    parts = taken([swapped(near)], running, True)
+    running = taken([others, far_same], running, False)
+    parts = taken([swapped(others)], running, True)
     parts = exchange(parts, GROUP)
     return pl.pallas_call(
         combine,

time: 104 us -> 102 us (0.981)
  waiting for transfers between devices: 9.74 us -> 1.82 us
  starting transfers between devices: 25.8 us -> 31.9 us
    ppermute x3, waiting for transfers between devices: 8.58 us -> 0.23 us  [moved(): lax.ppermute(value, ZX, [(place(x, z), place(x + along_x, z + along_z)) f...]
    ppermute x1 -> x2, starting transfers between devices: 8.39 us -> 14.4 us  [swapped(): return lax.ppermute(value, 'core', [(0, 1), (1, 0)])]
    pallas_call x2 -> x3, Pallas kernels: 7.03 us -> 7.14 us  [taken(): pl.pallas_call(functools.partial(classify, sharpness, len(row_parts), boo...]
  transfers between devices with their start and end apart: 5 -> 6, of which waited for: 4 -> 3; matrix products, arithmetic and copies ran while one was open for 0% -> 0% of each run, Pallas kernels for 3% -> 4%
where the time goes in v4:
time: 102 us
  blocking collectives  57.5 us (56%)
  starting transfers between devices  31.9 us (31%)
  Pallas kernels  8.11 us (8%)
  local copies, waits for them, and re-layouts  2.32 us (2%)
  waiting for transfers between devices  1.82 us (2%)
    all_gather x1, blocking collectives, shards(): same = lax.all_gather(rows, 'z_hi', axis=0, tiled=True)  34.1 us
    all_to_all x1, blocking collectives, exchange(): return lax.all_to_all(value, axes, 0, 0, tiled=True)  23.4 us
    ppermute x2, starting transfers between devices, swapped(): return lax.ppermute(value, 'core', [(0, 1), (1, 0)])  14.4 us
    ppermute x3, starting transfers between devices, moved(): lax.ppermute(value, ZX, [(place(x, z), place(x + along_x, z + along_z)) f...  9.93 us
    all_to_all x1, starting transfers between devices, exchange(): return lax.all_to_all(value, axes, 0, 0, tiled=True)  7.61 us
    pallas_call x3, Pallas kernels, taken(): pl.pallas_call(functools.partial(classify, sharpness, len(row_parts), boo...  7.14 us
    broadcast_in_dim x1, local copies, waits for them, and re-layouts, copies(): jnp.broadcast_to(value[None], (count, rows, width))  2.18 us
  transfers between devices with their start and end apart: 6, of which 3 were waited for; matrix products, arithmetic and copies ran while one was open for 0% of the time, Pallas kernels for 4%

profile of v4, /device:TPU:1, one launch (start us, length us, event | category | flops | bytes accessed | tf_op | source)
XLA Modules:
  0.0 101.8 jit_solution(17187618026867013475)
XLA Ops:
  0.0 2.2 %broadcast_in_dim.2 = bf16[8,128,768]{2,1,0:T(8,128)(2,1)} broadcast(bf16[128,768]{1,0:T(8,128)(2,1)} %param.3), dimensions={1,2} | broadcast | bytes 1769472 | tf_op jit(solution)/shard_map/broadcast_in_dim | solution.py:22
  2.2 0.0 copy-start
  2.2 0.0 copy-start.1
  2.2 7.6 %all-to-all-start = ((bf16[8,128,768]{2,1,0:T(8,128)(2,1)}), bf16[8,128,768]{2,1,0:T(8,128)(2,1)S(1)}, u32[]{:S(2)}, u32[]{:S(2)}) async-start(bf16[8,128,768]{2,1,0:T(8,128)(2,1)} %broadcast_in_dim.2), calls=%async_computation | async-start | bytes 3145728 | tf_op jit(solution)/shard_map/all_to_all | solution.py:26
  9.8 0.0 copy-done
  9.8 0.0 copy-done.1
  9.8 34.1 %all_gather.3.refs_0_ = bf16[256,1280]{1,0:T(8,128)(2,1)S(1)} all-gather(bf16[32,1280]{1,0:T(8,128)(2,1)S(1)} %pad_maximum_fusion), channel_id=1, replica_groups=mesh['x_lo'=2,'z_hi'=8,'z_lo'=2,'core'=2,'y'=4,'x_hi'=2] {'z_hi'}, dimensions={0}, use_global_device_ids=true | all-gather | bytes 737280 | tf_op jit(solution)/shard_map/all_gather | solution.py:156
  43.9 0.0 all-to-all-done
  43.9 3.4 %collective-permute-start.2 = (bf16[256,1280]{1,0:T(8,128)(2,1)S(1)}, bf16[256,1280]{1,0:T(8,128)(2,1)S(1)}, u32[]{:S(2)}, u32[]{:S(2)}) collective-permute-start(bf16[256,1280]{1,0:T(8,128)(2,1)S(1)} %all_gather.3.refs_0_), channel_id=1, source_target_pairs={{0,496},{16,256},{32,272},{48,288},{64,304},{80,320},{96,336},{112... | collective-permute-start | bytes 1966088 | tf_op jit(solution)/shard_map/ppermute | solution.py:37
  47.3 1.9 %collective-permute-start.1 = (bf16[256,1280]{1,0:T(8,128)(2,1)S(1)}, bf16[256,1280]{1,0:T(8,128)(2,1)S(1)}, u32[]{:S(2)}, u32[]{:S(2)}) collective-permute-start(bf16[256,1280]{1,0:T(8,128)(2,1)S(1)} %all_gather.3.refs_0_), channel_id=1, source_target_pairs={{0,16},{16,32},{32,48},{48,64},{64,80},{80,96},{96,112},{112,128},... | collective-permute-start | bytes 1966088 | tf_op jit(solution)/shard_map/ppermute | solution.py:37
  49.3 4.6 %collective-permute-start = (bf16[256,1280]{1,0:T(8,128)(2,1)S(1)}, bf16[256,1280]{1,0:T(8,128)(2,1)S(1)}, u32[]{:S(2)}, u32[]{:S(2)}) collective-permute-start(bf16[256,1280]{1,0:T(8,128)(2,1)S(1)} %all_gather.3.refs_0_), channel_id=1, source_target_pairs={{0,257},{16,273},{32,289},{48,305},{64,321},{80,337},{96,353},{112... | collective-permute-start | bytes 1966088 | tf_op jit(solution)/shard_map/ppermute | solution.py:37
  53.9 1.0 classify.3
  54.9 7.5 %collective-permute-start.3 = (bf16[256,1280]{1,0:T(8,128)(2,1)S(1)}, bf16[256,1280]{1,0:T(8,128)(2,1)S(1)}, u32[]{:S(2)}, u32[]{:S(2)}) collective-permute-start(bf16[256,1280]{1,0:T(8,128)(2,1)S(1)} %all_gather.3.refs_0_), channel_id=1, source_target_pairs={{0,8},{8,0},{1,9},{9,1},{2,10},{10,2},{3,11},{11,3},{4,12},{12,4},... | collective-permute-start | bytes 1966088 | tf_op jit(solution)/shard_map/ppermute | solution.py:49
  62.4 0.0 collective-permute-done.2
  62.4 0.0 collective-permute-done.1
  62.4 0.2 collective-permute-done
  62.6 1.5 %collective-permute-done.3.refs_1_ = bf16[256,1280]{1,0:T(8,128)(2,1)S(1)} collective-permute-done((bf16[256,1280]{1,0:T(8,128)(2,1)S(1)}, bf16[256,1280]{1,0:T(8,128)(2,1)S(1)}, u32[]{:S(2)}, u32[]{:S(2)}) %collective-permute-start.3) | collective-permute-done | bytes 655392 | tf_op jit(solution)/shard_map/ppermute | solution.py:49
  64.2 6.9 %collective-permute-start.4 = (bf16[768,1280]{1,0:T(8,128)(2,1)S(1)}, bf16[768,1280]{1,0:T(8,128)(2,1)S(1)}, u32[]{:S(2)}, u32[]{:S(2)}) collective-permute-start(bf16[768,1280]{1,0:T(8,128)(2,1)S(1)} %constant_dynamic-update-slice_fusion.refs_0_), channel_id=1, source_target_pairs={{0,8},{8,0},{1,9},{9,1},{2,10},{10,2},{3,11},{11,3},{4,12},{12,4},... | collective-permute-start | bytes 5898248 | tf_op jit(solution)/shard_map/ppermute | solution.py:49
  71.2 3.4 %classify.4 = (f32[512,1024]{1,0:T(8,128)S(1)}, f32[8,1024]{1,0:T(8,128)S(1)}) custom-call(bf16[768,1280]{1,0:T(8,128)(2,1)S(1)} %constant_dynamic-update-slice_fusion.refs_0_, bf16[256,1280]{1,0:T(8,128)(2,1)S(1)} %collective-permute-done.3.refs_1_, bf16[1024,768]{1,0:T(8,128)(2,1)S(1)} %bitcast.2, f32[512,1024]{1,0:T(8,128)S(1)} %get-tuple-element.27.refs_3_, ...), custom_call_target="tpu_custom_call" | custom-call | flops 2684354560 | bytes 4194304 | tf_op jit(solution)/shard_map/classify/pallas_call | solution.py:176
  74.6 0.1 collective-permute-done.4.refs_0_
  74.7 2.7 %classify.5 = bf16[8,528,128]{2,1,0:T(8,128)(2,1)S(1)} custom-call(bf16[768,1280]{1,0:T(8,128)(2,1)S(1)} %collective-permute-done.4.refs_0_, bf16[1024,768]{1,0:T(8,128)(2,1)S(1)} %bitcast.3, f32[512,1024]{1,0:T(8,128)S(1)} %get-tuple-element.29.refs_2_, f32[8,1024]{1,0:T(8,128)S(1)} %get-tuple-element.30.refs_3_), custom_call_target="tpu_custom_call" | custom-call | flops 2013265920 | bytes 4194304 | tf_op jit(solution)/shard_map/classify/pallas_call | solution.py:176
  77.4 23.4 %all_to_all.14.parts_ref = bf16[8,528,128]{2,1,0:T(8,128)(2,1)S(1)} all-to-all(bf16[8,528,128]{2,1,0:T(8,128)(2,1)S(1)} %classify.5), channel_id=1, replica_groups=mesh['x_lo'=2,'z_hi'=8,'z_lo'=2,'core'=2,'y'=4,'x_hi'=2] {'y','x_hi'}, dimensions={0} | all-to-all | bytes 2162688 | tf_op jit(solution)/shard_map/all_to_all | solution.py:26
  100.8 1.0 combine.1
  (4 shorter events, 0.1 us)
Async XLA Ops:
  2.2 7.6 %copy-start = (bf16[32,768]{1,0:T(8,128)(2,1)S(1)}, bf16[32,768]{1,0:T(8,128)(2,1)}, u32[]{:S(2)}) copy-start(bf16[32,768]{1,0:T(8,128)(2,1)} %param.4) | copy-start | bytes 147460
  2.2 7.6 %copy-start.1 = (bf16[32,512]{1,0:T(8,128)(2,1)S(1)}, bf16[32,512]{1,0:T(8,128)(2,1)}, u32[]{:S(2)}) copy-start(bf16[32,512]{1,0:T(8,128)(2,1)} %param.5) | copy-start | bytes 98308
  2.2 41.7 %all-to-all-start = ((bf16[8,128,768]{2,1,0:T(8,128)(2,1)}), bf16[8,128,768]{2,1,0:T(8,128)(2,1)S(1)}, u32[]{:S(2)}, u32[]{:S(2)}) async-start(bf16[8,128,768]{2,1,0:T(8,128)(2,1)} %broadcast_in_dim.2), calls=%async_computation | async-start | bytes 3145728 | tf_op jit(solution)/shard_map/all_to_all | solution.py:26
  43.9 18.4 %collective-permute-start.2 = (bf16[256,1280]{1,0:T(8,128)(2,1)S(1)}, bf16[256,1280]{1,0:T(8,128)(2,1)S(1)}, u32[]{:S(2)}, u32[]{:S(2)}) collective-permute-start(bf16[256,1280]{1,0:T(8,128)(2,1)S(1)} %all_gather.3.refs_0_), channel_id=1, source_target_pairs={{0,496},{16,256},{32,272},{48,288},{64,304},{80,320},{96,336},{112... | collective-permute-start | bytes 1966088 | tf_op jit(solution)/shard_map/ppermute | solution.py:37
  47.3 15.0 %collective-permute-start.1 = (bf16[256,1280]{1,0:T(8,128)(2,1)S(1)}, bf16[256,1280]{1,0:T(8,128)(2,1)S(1)}, u32[]{:S(2)}, u32[]{:S(2)}) collective-permute-start(bf16[256,1280]{1,0:T(8,128)(2,1)S(1)} %all_gather.3.refs_0_), channel_id=1, source_target_pairs={{0,16},{16,32},{32,48},{48,64},{64,80},{80,96},{96,112},{112,128},... | collective-permute-start | bytes 1966088 | tf_op jit(solution)/shard_map/ppermute | solution.py:37
  49.3 13.3 %collective-permute-start = (bf16[256,1280]{1,0:T(8,128)(2,1)S(1)}, bf16[256,1280]{1,0:T(8,128)(2,1)S(1)}, u32[]{:S(2)}, u32[]{:S(2)}) collective-permute-start(bf16[256,1280]{1,0:T(8,128)(2,1)S(1)} %all_gather.3.refs_0_), channel_id=1, source_target_pairs={{0,257},{16,273},{32,289},{48,305},{64,321},{80,337},{96,353},{112... | collective-permute-start | bytes 1966088 | tf_op jit(solution)/shard_map/ppermute | solution.py:37
  54.9 9.2 %collective-permute-start.3 = (bf16[256,1280]{1,0:T(8,128)(2,1)S(1)}, bf16[256,1280]{1,0:T(8,128)(2,1)S(1)}, u32[]{:S(2)}, u32[]{:S(2)}) collective-permute-start(bf16[256,1280]{1,0:T(8,128)(2,1)S(1)} %all_gather.3.refs_0_), channel_id=1, source_target_pairs={{0,8},{8,0},{1,9},{9,1},{2,10},{10,2},{3,11},{11,3},{4,12},{12,4},... | collective-permute-start | bytes 1966088 | tf_op jit(solution)/shard_map/ppermute | solution.py:49
  64.2 10.5 %collective-permute-start.4 = (bf16[768,1280]{1,0:T(8,128)(2,1)S(1)}, bf16[768,1280]{1,0:T(8,128)(2,1)S(1)}, u32[]{:S(2)}, u32[]{:S(2)}) collective-permute-start(bf16[768,1280]{1,0:T(8,128)(2,1)S(1)} %constant_dynamic-update-slice_fusion.refs_0_), channel_id=1, source_target_pairs={{0,8},{8,0},{1,9},{9,1},{2,10},{10,2},{3,11},{11,3},{4,12},{12,4},... | collective-permute-start | bytes 5898248 | tf_op jit(solution)/shard_map/ppermute | solution.py:49

commit v5 on v4

--- a/solution.py
+++ b/solution.py
@@ -88,12 +88,14 @@
             past_top = past_stats_ref[0:1, columns]
             top = jnp.maximum(top, past_top)
             fade = jnp.exp2((past_top - top) * rate)
-        weights = [jnp.exp2((part - top) * rate) for part in now]
-        total = sum(jnp.sum(part, axis=0, keepdims=True) for part in weights)
+        weights = [jnp.exp2((part - top) * rate).astype(jnp.bfloat16) for part in now]
+        total = sum(
+            jnp.sum(part.astype(jnp.float32), axis=0, keepdims=True) for part in weights
+        )
         weighted = sum(
             jnp.dot(
                 labels_ref[:, bounds[index] : bounds[index + 1]],
-                part.astype(jnp.bfloat16),
+                part,
                 preferred_element_type=jnp.float32,
             )
             for index, part in enumerate(weights)

time: 102 us -> 102 us (level)
  no operation moved by 1% of the time
where the time goes in v5:
time: 102 us
  blocking collectives  57.5 us (56%)
  starting transfers between devices  31.9 us (31%)
  Pallas kernels  8.21 us (8%)
  local copies, waits for them, and re-layouts  2.32 us (2%)
  waiting for transfers between devices  1.85 us (2%)
    all_gather x1, blocking collectives, shards(): same = lax.all_gather(rows, 'z_hi', axis=0, tiled=True)  34.1 us
    all_to_all x1, blocking collectives, exchange(): return lax.all_to_all(value, axes, 0, 0, tiled=True)  23.4 us
    ppermute x2, starting transfers between devices, swapped(): return lax.ppermute(value, 'core', [(0, 1), (1, 0)])  14.4 us
    ppermute x3, starting transfers between devices, moved(): lax.ppermute(value, ZX, [(place(x, z), place(x + along_x, z + along_z)) f...  9.93 us
    all_to_all x1, starting transfers between devices, exchange(): return lax.all_to_all(value, axes, 0, 0, tiled=True)  7.61 us
    pallas_call x3, Pallas kernels, taken(): pl.pallas_call(functools.partial(classify, sharpness, len(row_parts), boo...  7.24 us
    broadcast_in_dim x1, local copies, waits for them, and re-layouts, copies(): jnp.broadcast_to(value[None], (count, rows, width))  2.18 us
  transfers between devices with their start and end apart: 6, of which 3 were waited for; matrix products, arithmetic and copies ran while one was open for 0% of the time, Pallas kernels for 4%

profile of v5, /device:TPU:1, one launch (start us, length us, event | category | flops | bytes accessed | tf_op | source)
XLA Modules:
  0.0 101.9 jit_solution(10509675150500470881)
XLA Ops:
  0.0 2.2 %broadcast_in_dim.2 = bf16[8,128,768]{2,1,0:T(8,128)(2,1)} broadcast(bf16[128,768]{1,0:T(8,128)(2,1)} %param.3), dimensions={1,2} | broadcast | bytes 1769472 | tf_op jit(solution)/shard_map/broadcast_in_dim | solution.py:22
  2.2 0.0 copy-start
  2.2 0.0 copy-start.1
  2.2 7.6 %all-to-all-start = ((bf16[8,128,768]{2,1,0:T(8,128)(2,1)}), bf16[8,128,768]{2,1,0:T(8,128)(2,1)S(1)}, u32[]{:S(2)}, u32[]{:S(2)}) async-start(bf16[8,128,768]{2,1,0:T(8,128)(2,1)} %broadcast_in_dim.2), calls=%async_computation | async-start | bytes 3145728 | tf_op jit(solution)/shard_map/all_to_all | solution.py:26
  9.8 0.0 copy-done
  9.8 0.0 copy-done.1
  9.8 34.1 %all_gather.3.refs_0_ = bf16[256,1280]{1,0:T(8,128)(2,1)S(1)} all-gather(bf16[32,1280]{1,0:T(8,128)(2,1)S(1)} %pad_maximum_fusion), channel_id=1, replica_groups=mesh['x_lo'=2,'z_hi'=8,'z_lo'=2,'core'=2,'y'=4,'x_hi'=2] {'z_hi'}, dimensions={0}, use_global_device_ids=true | all-gather | bytes 737280 | tf_op jit(solution)/shard_map/all_gather | solution.py:158
  43.9 0.0 all-to-all-done
  43.9 3.4 %collective-permute-start.2 = (bf16[256,1280]{1,0:T(8,128)(2,1)S(1)}, bf16[256,1280]{1,0:T(8,128)(2,1)S(1)}, u32[]{:S(2)}, u32[]{:S(2)}) collective-permute-start(bf16[256,1280]{1,0:T(8,128)(2,1)S(1)} %all_gather.3.refs_0_), channel_id=1, source_target_pairs={{0,496},{16,256},{32,272},{48,288},{64,304},{80,320},{96,336},{112... | collective-permute-start | bytes 1966088 | tf_op jit(solution)/shard_map/ppermute | solution.py:37
  47.3 1.9 %collective-permute-start.1 = (bf16[256,1280]{1,0:T(8,128)(2,1)S(1)}, bf16[256,1280]{1,0:T(8,128)(2,1)S(1)}, u32[]{:S(2)}, u32[]{:S(2)}) collective-permute-start(bf16[256,1280]{1,0:T(8,128)(2,1)S(1)} %all_gather.3.refs_0_), channel_id=1, source_target_pairs={{0,16},{16,32},{32,48},{48,64},{64,80},{80,96},{96,112},{112,128},... | collective-permute-start | bytes 1966088 | tf_op jit(solution)/shard_map/ppermute | solution.py:37
  49.3 4.6 %collective-permute-start = (bf16[256,1280]{1,0:T(8,128)(2,1)S(1)}, bf16[256,1280]{1,0:T(8,128)(2,1)S(1)}, u32[]{:S(2)}, u32[]{:S(2)}) collective-permute-start(bf16[256,1280]{1,0:T(8,128)(2,1)S(1)} %all_gather.3.refs_0_), channel_id=1, source_target_pairs={{0,257},{16,273},{32,289},{48,305},{64,321},{80,337},{96,353},{112... | collective-permute-start | bytes 1966088 | tf_op jit(solution)/shard_map/ppermute | solution.py:37
  53.9 1.1 %classify.3 = (f32[512,1024]{1,0:T(8,128)S(1)}, f32[8,1024]{1,0:T(8,128)S(1)}) custom-call(bf16[256,1280]{1,0:T(8,128)(2,1)S(1)} %all_gather.3.refs_0_, bf16[1024,768]{1,0:T(8,128)(2,1)S(1)} %bitcast.1), custom_call_target="tpu_custom_call" | custom-call | flops 671088640 | bytes 4194304 | tf_op jit(solution)/shard_map/classify/pallas_call | solution.py:178
  54.9 7.5 %collective-permute-start.3 = (bf16[256,1280]{1,0:T(8,128)(2,1)S(1)}, bf16[256,1280]{1,0:T(8,128)(2,1)S(1)}, u32[]{:S(2)}, u32[]{:S(2)}) collective-permute-start(bf16[256,1280]{1,0:T(8,128)(2,1)S(1)} %all_gather.3.refs_0_), channel_id=1, source_target_pairs={{0,8},{8,0},{1,9},{9,1},{2,10},{10,2},{3,11},{11,3},{4,12},{12,4},... | collective-permute-start | bytes 1966088 | tf_op jit(solution)/shard_map/ppermute | solution.py:49
  62.4 0.0 collective-permute-done.2
  62.4 0.0 collective-permute-done.1
  62.4 0.2 collective-permute-done
  62.6 1.5 %collective-permute-done.3.refs_1_ = bf16[256,1280]{1,0:T(8,128)(2,1)S(1)} collective-permute-done((bf16[256,1280]{1,0:T(8,128)(2,1)S(1)}, bf16[256,1280]{1,0:T(8,128)(2,1)S(1)}, u32[]{:S(2)}, u32[]{:S(2)}) %collective-permute-start.3) | collective-permute-done | bytes 655392 | tf_op jit(solution)/shard_map/ppermute | solution.py:49
  64.2 6.9 %collective-permute-start.4 = (bf16[768,1280]{1,0:T(8,128)(2,1)S(1)}, bf16[768,1280]{1,0:T(8,128)(2,1)S(1)}, u32[]{:S(2)}, u32[]{:S(2)}) collective-permute-start(bf16[768,1280]{1,0:T(8,128)(2,1)S(1)} %constant_dynamic-update-slice_fusion.refs_0_), channel_id=1, source_target_pairs={{0,8},{8,0},{1,9},{9,1},{2,10},{10,2},{3,11},{11,3},{4,12},{12,4},... | collective-permute-start | bytes 5898248 | tf_op jit(solution)/shard_map/ppermute | solution.py:49
  71.2 3.4 %classify.4 = (f32[512,1024]{1,0:T(8,128)S(1)}, f32[8,1024]{1,0:T(8,128)S(1)}) custom-call(bf16[768,1280]{1,0:T(8,128)(2,1)S(1)} %constant_dynamic-update-slice_fusion.refs_0_, bf16[256,1280]{1,0:T(8,128)(2,1)S(1)} %collective-permute-done.3.refs_1_, bf16[1024,768]{1,0:T(8,128)(2,1)S(1)} %bitcast.2, f32[512,1024]{1,0:T(8,128)S(1)} %get-tuple-element.27.refs_3_, ...), custom_call_target="tpu_custom_call" | custom-call | flops 2684354560 | bytes 4194304 | tf_op jit(solution)/shard_map/classify/pallas_call | solution.py:178
  74.6 0.2 collective-permute-done.4.refs_0_
  74.7 2.8 %classify.5 = bf16[8,528,128]{2,1,0:T(8,128)(2,1)S(1)} custom-call(bf16[768,1280]{1,0:T(8,128)(2,1)S(1)} %collective-permute-done.4.refs_0_, bf16[1024,768]{1,0:T(8,128)(2,1)S(1)} %bitcast.3, f32[512,1024]{1,0:T(8,128)S(1)} %get-tuple-element.29.refs_2_, f32[8,1024]{1,0:T(8,128)S(1)} %get-tuple-element.30.refs_3_), custom_call_target="tpu_custom_call" | custom-call | flops 2013265920 | bytes 4194304 | tf_op jit(solution)/shard_map/classify/pallas_call | solution.py:178
  77.5 23.4 %all_to_all.14.parts_ref = bf16[8,528,128]{2,1,0:T(8,128)(2,1)S(1)} all-to-all(bf16[8,528,128]{2,1,0:T(8,128)(2,1)S(1)} %classify.5), channel_id=1, replica_groups=mesh['x_lo'=2,'z_hi'=8,'z_lo'=2,'core'=2,'y'=4,'x_hi'=2] {'y','x_hi'}, dimensions={0} | all-to-all | bytes 2162688 | tf_op jit(solution)/shard_map/all_to_all | solution.py:26
  100.9 1.0 combine.1
  (4 shorter events, 0.1 us)
Async XLA Ops:
  2.2 7.6 %copy-start = (bf16[32,768]{1,0:T(8,128)(2,1)S(1)}, bf16[32,768]{1,0:T(8,128)(2,1)}, u32[]{:S(2)}) copy-start(bf16[32,768]{1,0:T(8,128)(2,1)} %param.4) | copy-start | bytes 147460
  2.2 7.6 %copy-start.1 = (bf16[32,512]{1,0:T(8,128)(2,1)S(1)}, bf16[32,512]{1,0:T(8,128)(2,1)}, u32[]{:S(2)}) copy-start(bf16[32,512]{1,0:T(8,128)(2,1)} %param.5) | copy-start | bytes 98308
  2.2 41.7 %all-to-all-start = ((bf16[8,128,768]{2,1,0:T(8,128)(2,1)}), bf16[8,128,768]{2,1,0:T(8,128)(2,1)S(1)}, u32[]{:S(2)}, u32[]{:S(2)}) async-start(bf16[8,128,768]{2,1,0:T(8,128)(2,1)} %broadcast_in_dim.2), calls=%async_computation | async-start | bytes 3145728 | tf_op jit(solution)/shard_map/all_to_all | solution.py:26
  43.9 18.5 %collective-permute-start.2 = (bf16[256,1280]{1,0:T(8,128)(2,1)S(1)}, bf16[256,1280]{1,0:T(8,128)(2,1)S(1)}, u32[]{:S(2)}, u32[]{:S(2)}) collective-permute-start(bf16[256,1280]{1,0:T(8,128)(2,1)S(1)} %all_gather.3.refs_0_), channel_id=1, source_target_pairs={{0,496},{16,256},{32,272},{48,288},{64,304},{80,320},{96,336},{112... | collective-permute-start | bytes 1966088 | tf_op jit(solution)/shard_map/ppermute | solution.py:37
  47.3 15.1 %collective-permute-start.1 = (bf16[256,1280]{1,0:T(8,128)(2,1)S(1)}, bf16[256,1280]{1,0:T(8,128)(2,1)S(1)}, u32[]{:S(2)}, u32[]{:S(2)}) collective-permute-start(bf16[256,1280]{1,0:T(8,128)(2,1)S(1)} %all_gather.3.refs_0_), channel_id=1, source_target_pairs={{0,16},{16,32},{32,48},{48,64},{64,80},{80,96},{96,112},{112,128},... | collective-permute-start | bytes 1966088 | tf_op jit(solution)/shard_map/ppermute | solution.py:37
  49.3 13.3 %collective-permute-start = (bf16[256,1280]{1,0:T(8,128)(2,1)S(1)}, bf16[256,1280]{1,0:T(8,128)(2,1)S(1)}, u32[]{:S(2)}, u32[]{:S(2)}) collective-permute-start(bf16[256,1280]{1,0:T(8,128)(2,1)S(1)} %all_gather.3.refs_0_), channel_id=1, source_target_pairs={{0,257},{16,273},{32,289},{48,305},{64,321},{80,337},{96,353},{112... | collective-permute-start | bytes 1966088 | tf_op jit(solution)/shard_map/ppermute | solution.py:37
  54.9 9.2 %collective-permute-start.3 = (bf16[256,1280]{1,0:T(8,128)(2,1)S(1)}, bf16[256,1280]{1,0:T(8,128)(2,1)S(1)}, u32[]{:S(2)}, u32[]{:S(2)}) collective-permute-start(bf16[256,1280]{1,0:T(8,128)(2,1)S(1)} %all_gather.3.refs_0_), channel_id=1, source_target_pairs={{0,8},{8,0},{1,9},{9,1},{2,10},{10,2},{3,11},{11,3},{4,12},{12,4},... | collective-permute-start | bytes 1966088 | tf_op jit(solution)/shard_map/ppermute | solution.py:49
  64.2 10.5 %collective-permute-start.4 = (bf16[768,1280]{1,0:T(8,128)(2,1)S(1)}, bf16[768,1280]{1,0:T(8,128)(2,1)S(1)}, u32[]{:S(2)}, u32[]{:S(2)}) collective-permute-start(bf16[768,1280]{1,0:T(8,128)(2,1)S(1)} %constant_dynamic-update-slice_fusion.refs_0_), channel_id=1, source_target_pairs={{0,8},{8,0},{1,9},{9,1},{2,10},{10,2},{3,11},{11,3},{4,12},{12,4},... | collective-permute-start | bytes 5898248 | tf_op jit(solution)/shard_map/ppermute | solution.py:49

commit v6 on v5

--- a/solution.py
+++ b/solution.py
@@ -11,7 +11,7 @@
 
 AXES = ("x_lo", "z_hi", "z_lo", "core", "y", "x_hi")
 SIZES = (2, 8, 2, 2, 4, 2)
-ZX = ("x_lo", "z_hi", "z_lo", "x_hi")
+ZX = ("x_lo", "z_hi", "z_lo", "core", "x_hi")
 GROUP = ("y", "x_hi")
 EXTRA = 16
 STEP = 512
@@ -30,15 +30,16 @@
     columns = lax.axis_size("x_lo") * lax.axis_size("x_hi")
     height = lax.axis_size("z_hi") * lax.axis_size("z_lo")
 
-    def place(x, z):
+    def place(x, z, core):
         x, z = x % columns, z % height
-        return ((x % 2) * height + z) * 2 + x // 2
+        return (((x % 2) * height + z) * 2 + core) * 2 + x // 2
 
     return lax.ppermute(
         value,
         ZX,
         [
-            (place(x, z), place(x + along_x, z + along_z))
+            (place(x, z, core), place(x + sign * along_x, z + sign * along_z, core))
+            for core, sign in ((0, 1), (1, -1))
             for x in range(columns)
             for z in range(height)
         ],

time: 102 us -> 103 us (level)
  waiting for transfers between devices: 1.85 us -> 9.25 us
  starting transfers between devices: 31.9 us -> 26.9 us
  blocking collectives: 57.5 us -> 55.4 us
    ppermute x3, waiting for transfers between devices: 0.19 us -> 8.73 us  [moved(): lax.ppermute(value, ZX, [(place(x, z, core), place(x + sign * along_x, z...]
    ppermute x2, starting transfers between devices: 14.4 us -> 8.48 us  [swapped(): return lax.ppermute(value, 'core', [(0, 1), (1, 0)])]
    all_to_all x1, blocking collectives: 23.4 us -> 21.3 us  [exchange(): return lax.all_to_all(value, axes, 0, 0, tiled=True)]
    ppermute x2, waiting for transfers between devices: 1.65 us -> 0.51 us  [swapped(): return lax.ppermute(value, 'core', [(0, 1), (1, 0)])]
where the time goes in v6:
time: 103 us; the launch traced here: 102 us
  blocking collectives  55.4 us (54%)
  starting transfers between devices  26.9 us (26%)
  waiting for transfers between devices  9.25 us (9%)
  Pallas kernels  8.22 us (8%)
  local copies, waits for them, and re-layouts  2.32 us (2%)
    all_gather x1, blocking collectives, shards(): same = lax.all_gather(rows, 'z_hi', axis=0, tiled=True)  34.1 us
    all_to_all x1, blocking collectives, exchange(): return lax.all_to_all(value, axes, 0, 0, tiled=True)  21.3 us
    ppermute x3, starting transfers between devices, moved(): lax.ppermute(value, ZX, [(place(x, z, core), place(x + sign * along_x, z...  10.8 us
    ppermute x3, waiting for transfers between devices, moved(): lax.ppermute(value, ZX, [(place(x, z, core), place(x + sign * along_x, z...  8.73 us
    ppermute x2, starting transfers between devices, swapped(): return lax.ppermute(value, 'core', [(0, 1), (1, 0)])  8.48 us
    all_to_all x1, starting transfers between devices, exchange(): return lax.all_to_all(value, axes, 0, 0, tiled=True)  7.61 us
    pallas_call x3, Pallas kernels, taken(): pl.pallas_call(functools.partial(classify, sharpness, len(row_parts), boo...  7.25 us
    broadcast_in_dim x1, local copies, waits for them, and re-layouts, copies(): jnp.broadcast_to(value[None], (count, rows, width))  2.18 us
  transfers between devices with their start and end apart: 6, of which 3 were waited for; matrix products, arithmetic and copies ran while one was open for 0% of the time, Pallas kernels for 4%

profile of v6, /device:TPU:1, one launch (start us, length us, event | category | flops | bytes accessed | tf_op | source)
XLA Modules:
  0.0 102.2 jit_solution(4025593916960955434)
XLA Ops:
  0.0 2.2 %broadcast_in_dim.2 = bf16[8,128,768]{2,1,0:T(8,128)(2,1)} broadcast(bf16[128,768]{1,0:T(8,128)(2,1)} %param.3), dimensions={1,2} | broadcast | bytes 1769472 | tf_op jit(solution)/shard_map/broadcast_in_dim | solution.py:22
  2.2 0.0 copy-start
  2.2 0.0 copy-start.1
  2.2 7.6 %all-to-all-start = ((bf16[8,128,768]{2,1,0:T(8,128)(2,1)}), bf16[8,128,768]{2,1,0:T(8,128)(2,1)S(1)}, u32[]{:S(2)}, u32[]{:S(2)}) async-start(bf16[8,128,768]{2,1,0:T(8,128)(2,1)} %broadcast_in_dim.2), calls=%async_computation | async-start | bytes 3145728 | tf_op jit(solution)/shard_map/all_to_all | solution.py:26
  9.8 0.0 copy-done
  9.8 0.0 copy-done.1
  9.8 34.1 %all_gather.3.refs_0_ = bf16[256,1280]{1,0:T(8,128)(2,1)S(1)} all-gather(bf16[32,1280]{1,0:T(8,128)(2,1)S(1)} %pad_maximum_fusion), channel_id=1, replica_groups=mesh['x_lo'=2,'z_hi'=8,'z_lo'=2,'core'=2,'y'=4,'x_hi'=2] {'z_hi'}, dimensions={0}, use_global_device_ids=true | all-gather | bytes 737280 | tf_op jit(solution)/shard_map/all_gather | solution.py:159
  43.9 0.0 all-to-all-done
  43.9 4.9 %collective-permute-start.2 = (bf16[256,1280]{1,0:T(8,128)(2,1)S(1)}, bf16[256,1280]{1,0:T(8,128)(2,1)S(1)}, u32[]{:S(2)}, u32[]{:S(2)}) collective-permute-start(bf16[256,1280]{1,0:T(8,128)(2,1)S(1)} %all_gather.3.refs_0_), channel_id=1, source_target_pairs={{0,496},{16,256},{32,272},{48,288},{64,304},{80,320},{96,336},{112... | collective-permute-start | bytes 1966088 | tf_op jit(solution)/shard_map/ppermute | solution.py:37
  48.9 4.0 %collective-permute-start.1 = (bf16[256,1280]{1,0:T(8,128)(2,1)S(1)}, bf16[256,1280]{1,0:T(8,128)(2,1)S(1)}, u32[]{:S(2)}, u32[]{:S(2)}) collective-permute-start(bf16[256,1280]{1,0:T(8,128)(2,1)S(1)} %all_gather.3.refs_0_), channel_id=1, source_target_pairs={{0,16},{16,32},{32,48},{48,64},{64,80},{80,96},{96,112},{112,128},... | collective-permute-start | bytes 1966088 | tf_op jit(solution)/shard_map/ppermute | solution.py:37
  52.8 1.9 %collective-permute-start = (bf16[256,1280]{1,0:T(8,128)(2,1)S(1)}, bf16[256,1280]{1,0:T(8,128)(2,1)S(1)}, u32[]{:S(2)}, u32[]{:S(2)}) collective-permute-start(bf16[256,1280]{1,0:T(8,128)(2,1)S(1)} %all_gather.3.refs_0_), channel_id=1, source_target_pairs={{0,257},{16,273},{32,289},{48,305},{64,321},{80,337},{96,353},{112... | collective-permute-start | bytes 1966088 | tf_op jit(solution)/shard_map/ppermute | solution.py:37
  54.8 1.1 %classify.3 = (f32[512,1024]{1,0:T(8,128)S(1)}, f32[8,1024]{1,0:T(8,128)S(1)}) custom-call(bf16[256,1280]{1,0:T(8,128)(2,1)S(1)} %all_gather.3.refs_0_, bf16[1024,768]{1,0:T(8,128)(2,1)S(1)} %bitcast.1), custom_call_target="tpu_custom_call" | custom-call | flops 671088640 | bytes 4194304 | tf_op jit(solution)/shard_map/classify/pallas_call | solution.py:179
  55.8 6.6 %collective-permute-start.3 = (bf16[256,1280]{1,0:T(8,128)(2,1)S(1)}, bf16[256,1280]{1,0:T(8,128)(2,1)S(1)}, u32[]{:S(2)}, u32[]{:S(2)}) collective-permute-start(bf16[256,1280]{1,0:T(8,128)(2,1)S(1)} %all_gather.3.refs_0_), channel_id=1, source_target_pairs={{0,8},{8,0},{1,9},{9,1},{2,10},{10,2},{3,11},{11,3},{4,12},{12,4},... | collective-permute-start | bytes 1966088 | tf_op jit(solution)/shard_map/ppermute | solution.py:50
  62.4 0.0 collective-permute-done.2
  62.4 5.0 %collective-permute-done.1 = bf16[256,1280]{1,0:T(8,128)(2,1)S(1)} collective-permute-done((bf16[256,1280]{1,0:T(8,128)(2,1)S(1)}, bf16[256,1280]{1,0:T(8,128)(2,1)S(1)}, u32[]{:S(2)}, u32[]{:S(2)}) %collective-permute-start.1) | collective-permute-done | bytes 655392 | tf_op jit(solution)/shard_map/ppermute | solution.py:37
  67.4 3.7 %collective-permute-done = bf16[256,1280]{1,0:T(8,128)(2,1)S(1)} collective-permute-done((bf16[256,1280]{1,0:T(8,128)(2,1)S(1)}, bf16[256,1280]{1,0:T(8,128)(2,1)S(1)}, u32[]{:S(2)}, u32[]{:S(2)}) %collective-permute-start) | collective-permute-done | bytes 655392 | tf_op jit(solution)/shard_map/ppermute | solution.py:37
  71.1 0.0 collective-permute-done.3.refs_1_
  71.3 1.9 %collective-permute-start.4 = (bf16[768,1280]{1,0:T(8,128)(2,1)S(1)}, bf16[768,1280]{1,0:T(8,128)(2,1)S(1)}, u32[]{:S(2)}, u32[]{:S(2)}) collective-permute-start(bf16[768,1280]{1,0:T(8,128)(2,1)S(1)} %constant_dynamic-update-slice_fusion.refs_0_), channel_id=1, source_target_pairs={{0,8},{8,0},{1,9},{9,1},{2,10},{10,2},{3,11},{11,3},{4,12},{12,4},... | collective-permute-start | bytes 5898248 | tf_op jit(solution)/shard_map/ppermute | solution.py:50
  73.2 3.4 %classify.4 = (f32[512,1024]{1,0:T(8,128)S(1)}, f32[8,1024]{1,0:T(8,128)S(1)}) custom-call(bf16[768,1280]{1,0:T(8,128)(2,1)S(1)} %constant_dynamic-update-slice_fusion.refs_0_, bf16[256,1280]{1,0:T(8,128)(2,1)S(1)} %collective-permute-done.3.refs_1_, bf16[1024,768]{1,0:T(8,128)(2,1)S(1)} %bitcast.2, f32[512,1024]{1,0:T(8,128)S(1)} %get-tuple-element.27.refs_3_, ...), custom_call_target="tpu_custom_call" | custom-call | flops 2684354560 | bytes 4194304 | tf_op jit(solution)/shard_map/classify/pallas_call | solution.py:179
  76.6 0.5 collective-permute-done.4.refs_0_
  77.2 2.8 %classify.5 = bf16[8,528,128]{2,1,0:T(8,128)(2,1)S(1)} custom-call(bf16[768,1280]{1,0:T(8,128)(2,1)S(1)} %collective-permute-done.4.refs_0_, bf16[1024,768]{1,0:T(8,128)(2,1)S(1)} %bitcast.3, f32[512,1024]{1,0:T(8,128)S(1)} %get-tuple-element.29.refs_2_, f32[8,1024]{1,0:T(8,128)S(1)} %get-tuple-element.30.refs_3_), custom_call_target="tpu_custom_call" | custom-call | flops 2013265920 | bytes 4194304 | tf_op jit(solution)/shard_map/classify/pallas_call | solution.py:179
  79.9 21.3 %all_to_all.14.parts_ref = bf16[8,528,128]{2,1,0:T(8,128)(2,1)S(1)} all-to-all(bf16[8,528,128]{2,1,0:T(8,128)(2,1)S(1)} %classify.5), channel_id=1, replica_groups=mesh['x_lo'=2,'z_hi'=8,'z_lo'=2,'core'=2,'y'=4,'x_hi'=2] {'y','x_hi'}, dimensions={0} | all-to-all | bytes 2162688 | tf_op jit(solution)/shard_map/all_to_all | solution.py:26
  101.3 1.0 combine.1
  (4 shorter events, 0.1 us)
Async XLA Ops:
  2.2 7.6 %copy-start = (bf16[32,768]{1,0:T(8,128)(2,1)S(1)}, bf16[32,768]{1,0:T(8,128)(2,1)}, u32[]{:S(2)}) copy-start(bf16[32,768]{1,0:T(8,128)(2,1)} %param.4) | copy-start | bytes 147460
  2.2 7.6 %copy-start.1 = (bf16[32,512]{1,0:T(8,128)(2,1)S(1)}, bf16[32,512]{1,0:T(8,128)(2,1)}, u32[]{:S(2)}) copy-start(bf16[32,512]{1,0:T(8,128)(2,1)} %param.5) | copy-start | bytes 98308
  2.2 41.7 %all-to-all-start = ((bf16[8,128,768]{2,1,0:T(8,128)(2,1)}), bf16[8,128,768]{2,1,0:T(8,128)(2,1)S(1)}, u32[]{:S(2)}, u32[]{:S(2)}) async-start(bf16[8,128,768]{2,1,0:T(8,128)(2,1)} %broadcast_in_dim.2), calls=%async_computation | async-start | bytes 3145728 | tf_op jit(solution)/shard_map/all_to_all | solution.py:26
  43.9 18.5 %collective-permute-start.2 = (bf16[256,1280]{1,0:T(8,128)(2,1)S(1)}, bf16[256,1280]{1,0:T(8,128)(2,1)S(1)}, u32[]{:S(2)}, u32[]{:S(2)}) collective-permute-start(bf16[256,1280]{1,0:T(8,128)(2,1)S(1)} %all_gather.3.refs_0_), channel_id=1, source_target_pairs={{0,496},{16,256},{32,272},{48,288},{64,304},{80,320},{96,336},{112... | collective-permute-start | bytes 1966088 | tf_op jit(solution)/shard_map/ppermute | solution.py:37
  48.9 18.5 %collective-permute-start.1 = (bf16[256,1280]{1,0:T(8,128)(2,1)S(1)}, bf16[256,1280]{1,0:T(8,128)(2,1)S(1)}, u32[]{:S(2)}, u32[]{:S(2)}) collective-permute-start(bf16[256,1280]{1,0:T(8,128)(2,1)S(1)} %all_gather.3.refs_0_), channel_id=1, source_target_pairs={{0,16},{16,32},{32,48},{48,64},{64,80},{80,96},{96,112},{112,128},... | collective-permute-start | bytes 1966088 | tf_op jit(solution)/shard_map/ppermute | solution.py:37
  52.8 18.3 %collective-permute-start = (bf16[256,1280]{1,0:T(8,128)(2,1)S(1)}, bf16[256,1280]{1,0:T(8,128)(2,1)S(1)}, u32[]{:S(2)}, u32[]{:S(2)}) collective-permute-start(bf16[256,1280]{1,0:T(8,128)(2,1)S(1)} %all_gather.3.refs_0_), channel_id=1, source_target_pairs={{0,257},{16,273},{32,289},{48,305},{64,321},{80,337},{96,353},{112... | collective-permute-start | bytes 1966088 | tf_op jit(solution)/shard_map/ppermute | solution.py:37
  55.8 15.3 %collective-permute-start.3 = (bf16[256,1280]{1,0:T(8,128)(2,1)S(1)}, bf16[256,1280]{1,0:T(8,128)(2,1)S(1)}, u32[]{:S(2)}, u32[]{:S(2)}) collective-permute-start(bf16[256,1280]{1,0:T(8,128)(2,1)S(1)} %all_gather.3.refs_0_), channel_id=1, source_target_pairs={{0,8},{8,0},{1,9},{9,1},{2,10},{10,2},{3,11},{11,3},{4,12},{12,4},... | collective-permute-start | bytes 1966088 | tf_op jit(solution)/shard_map/ppermute | solution.py:50
  71.3 5.9 %collective-permute-start.4 = (bf16[768,1280]{1,0:T(8,128)(2,1)S(1)}, bf16[768,1280]{1,0:T(8,128)(2,1)S(1)}, u32[]{:S(2)}, u32[]{:S(2)}) collective-permute-start(bf16[768,1280]{1,0:T(8,128)(2,1)S(1)} %constant_dynamic-update-slice_fusion.refs_0_), channel_id=1, source_target_pairs={{0,8},{8,0},{1,9},{9,1},{2,10},{10,2},{3,11},{11,3},{4,12},{12,4},... | collective-permute-start | bytes 5898248 | tf_op jit(solution)/shard_map/ppermute | solution.py:50

commit v7 on v5

--- a/solution.py
+++ b/solution.py
@@ -14,7 +14,7 @@
 ZX = ("x_lo", "z_hi", "z_lo", "x_hi")
 GROUP = ("y", "x_hi")
 EXTRA = 16
-STEP = 512
+STEP = 1024
 
 
 def copies(value, count):

time: 102 us -> 102 us (level)
  no operation moved by 1% of the time
where the time goes in v7:
time: 102 us
  blocking collectives  57.5 us (56%)
  starting transfers between devices  31.9 us (31%)
  Pallas kernels  8.21 us (8%)
  local copies, waits for them, and re-layouts  2.32 us (2%)
  waiting for transfers between devices  1.87 us (2%)
    all_gather x1, blocking collectives, shards(): same = lax.all_gather(rows, 'z_hi', axis=0, tiled=True)  34.1 us
    all_to_all x1, blocking collectives, exchange(): return lax.all_to_all(value, axes, 0, 0, tiled=True)  23.4 us
    ppermute x2, starting transfers between devices, swapped(): return lax.ppermute(value, 'core', [(0, 1), (1, 0)])  14.4 us
    ppermute x3, starting transfers between devices, moved(): lax.ppermute(value, ZX, [(place(x, z), place(x + along_x, z + along_z)) f...  9.93 us
    all_to_all x1, starting transfers between devices, exchange(): return lax.all_to_all(value, axes, 0, 0, tiled=True)  7.61 us
    pallas_call x3, Pallas kernels, taken(): pl.pallas_call(functools.partial(classify, sharpness, len(row_parts), boo...  7.25 us
    broadcast_in_dim x1, local copies, waits for them, and re-layouts, copies(): jnp.broadcast_to(value[None], (count, rows, width))  2.18 us
  transfers between devices with their start and end apart: 6, of which 3 were waited for; matrix products, arithmetic and copies ran while one was open for 0% of the time, Pallas kernels for 4%

profile of v7, /device:TPU:1, one launch (start us, length us, event | category | flops | bytes accessed | tf_op | source)
XLA Modules:
  0.0 101.9 jit_solution(13346458174316168294)
XLA Ops:
  0.0 2.2 %broadcast_in_dim.2 = bf16[8,128,768]{2,1,0:T(8,128)(2,1)} broadcast(bf16[128,768]{1,0:T(8,128)(2,1)} %param.3), dimensions={1,2} | broadcast | bytes 1769472 | tf_op jit(solution)/shard_map/broadcast_in_dim | solution.py:22
  2.2 0.0 copy-start
  2.2 0.0 copy-start.1
  2.2 7.6 %all-to-all-start = ((bf16[8,128,768]{2,1,0:T(8,128)(2,1)}), bf16[8,128,768]{2,1,0:T(8,128)(2,1)S(1)}, u32[]{:S(2)}, u32[]{:S(2)}) async-start(bf16[8,128,768]{2,1,0:T(8,128)(2,1)} %broadcast_in_dim.2), calls=%async_computation | async-start | bytes 3145728 | tf_op jit(solution)/shard_map/all_to_all | solution.py:26
  9.8 0.0 copy-done
  9.8 0.0 copy-done.1
  9.8 34.1 %all_gather.3.refs_0_ = bf16[256,1280]{1,0:T(8,128)(2,1)S(1)} all-gather(bf16[32,1280]{1,0:T(8,128)(2,1)S(1)} %pad_maximum_fusion), channel_id=1, replica_groups=mesh['x_lo'=2,'z_hi'=8,'z_lo'=2,'core'=2,'y'=4,'x_hi'=2] {'z_hi'}, dimensions={0}, use_global_device_ids=true | all-gather | bytes 737280 | tf_op jit(solution)/shard_map/all_gather | solution.py:158
  43.9 0.0 all-to-all-done
  43.9 3.4 %collective-permute-start.2 = (bf16[256,1280]{1,0:T(8,128)(2,1)S(1)}, bf16[256,1280]{1,0:T(8,128)(2,1)S(1)}, u32[]{:S(2)}, u32[]{:S(2)}) collective-permute-start(bf16[256,1280]{1,0:T(8,128)(2,1)S(1)} %all_gather.3.refs_0_), channel_id=1, source_target_pairs={{0,496},{16,256},{32,272},{48,288},{64,304},{80,320},{96,336},{112... | collective-permute-start | bytes 1966088 | tf_op jit(solution)/shard_map/ppermute | solution.py:37
  47.3 1.9 %collective-permute-start.1 = (bf16[256,1280]{1,0:T(8,128)(2,1)S(1)}, bf16[256,1280]{1,0:T(8,128)(2,1)S(1)}, u32[]{:S(2)}, u32[]{:S(2)}) collective-permute-start(bf16[256,1280]{1,0:T(8,128)(2,1)S(1)} %all_gather.3.refs_0_), channel_id=1, source_target_pairs={{0,16},{16,32},{32,48},{48,64},{64,80},{80,96},{96,112},{112,128},... | collective-permute-start | bytes 1966088 | tf_op jit(solution)/shard_map/ppermute | solution.py:37
  49.3 4.6 %collective-permute-start = (bf16[256,1280]{1,0:T(8,128)(2,1)S(1)}, bf16[256,1280]{1,0:T(8,128)(2,1)S(1)}, u32[]{:S(2)}, u32[]{:S(2)}) collective-permute-start(bf16[256,1280]{1,0:T(8,128)(2,1)S(1)} %all_gather.3.refs_0_), channel_id=1, source_target_pairs={{0,257},{16,273},{32,289},{48,305},{64,321},{80,337},{96,353},{112... | collective-permute-start | bytes 1966088 | tf_op jit(solution)/shard_map/ppermute | solution.py:37
  53.9 1.0 %classify.3 = (f32[512,1024]{1,0:T(8,128)S(1)}, f32[8,1024]{1,0:T(8,128)S(1)}) custom-call(bf16[256,1280]{1,0:T(8,128)(2,1)S(1)} %all_gather.3.refs_0_, bf16[1024,768]{1,0:T(8,128)(2,1)S(1)} %bitcast.1), custom_call_target="tpu_custom_call" | custom-call | flops 671088640 | bytes 4194304 | tf_op jit(solution)/shard_map/classify/pallas_call | solution.py:178
  54.9 7.5 %collective-permute-start.3 = (bf16[256,1280]{1,0:T(8,128)(2,1)S(1)}, bf16[256,1280]{1,0:T(8,128)(2,1)S(1)}, u32[]{:S(2)}, u32[]{:S(2)}) collective-permute-start(bf16[256,1280]{1,0:T(8,128)(2,1)S(1)} %all_gather.3.refs_0_), channel_id=1, source_target_pairs={{0,8},{8,0},{1,9},{9,1},{2,10},{10,2},{3,11},{11,3},{4,12},{12,4},... | collective-permute-start | bytes 1966088 | tf_op jit(solution)/shard_map/ppermute | solution.py:49
  62.4 0.0 collective-permute-done.2
  62.4 0.0 collective-permute-done.1
  62.4 0.2 collective-permute-done
  62.6 1.5 %collective-permute-done.3.refs_1_ = bf16[256,1280]{1,0:T(8,128)(2,1)S(1)} collective-permute-done((bf16[256,1280]{1,0:T(8,128)(2,1)S(1)}, bf16[256,1280]{1,0:T(8,128)(2,1)S(1)}, u32[]{:S(2)}, u32[]{:S(2)}) %collective-permute-start.3) | collective-permute-done | bytes 655392 | tf_op jit(solution)/shard_map/ppermute | solution.py:49
  64.2 6.9 %collective-permute-start.4 = (bf16[768,1280]{1,0:T(8,128)(2,1)S(1)}, bf16[768,1280]{1,0:T(8,128)(2,1)S(1)}, u32[]{:S(2)}, u32[]{:S(2)}) collective-permute-start(bf16[768,1280]{1,0:T(8,128)(2,1)S(1)} %constant_dynamic-update-slice_fusion.refs_0_), channel_id=1, source_target_pairs={{0,8},{8,0},{1,9},{9,1},{2,10},{10,2},{3,11},{11,3},{4,12},{12,4},... | collective-permute-start | bytes 5898248 | tf_op jit(solution)/shard_map/ppermute | solution.py:49
  71.2 3.4 %classify.4 = (f32[512,1024]{1,0:T(8,128)S(1)}, f32[8,1024]{1,0:T(8,128)S(1)}) custom-call(bf16[768,1280]{1,0:T(8,128)(2,1)S(1)} %constant_dynamic-update-slice_fusion.refs_0_, bf16[256,1280]{1,0:T(8,128)(2,1)S(1)} %collective-permute-done.3.refs_1_, bf16[1024,768]{1,0:T(8,128)(2,1)S(1)} %bitcast.2, f32[512,1024]{1,0:T(8,128)S(1)} %get-tuple-element.27.refs_3_, ...), custom_call_target="tpu_custom_call" | custom-call | flops 2684354560 | bytes 4194304 | tf_op jit(solution)/shard_map/classify/pallas_call | solution.py:178
  74.5 0.2 collective-permute-done.4.refs_0_
  74.7 2.8 %classify.5 = bf16[8,528,128]{2,1,0:T(8,128)(2,1)S(1)} custom-call(bf16[768,1280]{1,0:T(8,128)(2,1)S(1)} %collective-permute-done.4.refs_0_, bf16[1024,768]{1,0:T(8,128)(2,1)S(1)} %bitcast.3, f32[512,1024]{1,0:T(8,128)S(1)} %get-tuple-element.29.refs_2_, f32[8,1024]{1,0:T(8,128)S(1)} %get-tuple-element.30.refs_3_), custom_call_target="tpu_custom_call" | custom-call | flops 2013265920 | bytes 4194304 | tf_op jit(solution)/shard_map/classify/pallas_call | solution.py:178
  77.5 23.4 %all_to_all.14.parts_ref = bf16[8,528,128]{2,1,0:T(8,128)(2,1)S(1)} all-to-all(bf16[8,528,128]{2,1,0:T(8,128)(2,1)S(1)} %classify.5), channel_id=1, replica_groups=mesh['x_lo'=2,'z_hi'=8,'z_lo'=2,'core'=2,'y'=4,'x_hi'=2] {'y','x_hi'}, dimensions={0} | all-to-all | bytes 2162688 | tf_op jit(solution)/shard_map/all_to_all | solution.py:26
  101.0 1.0 combine.1
  (4 shorter events, 0.1 us)
Async XLA Ops:
  2.2 7.6 %copy-start = (bf16[32,768]{1,0:T(8,128)(2,1)S(1)}, bf16[32,768]{1,0:T(8,128)(2,1)}, u32[]{:S(2)}) copy-start(bf16[32,768]{1,0:T(8,128)(2,1)} %param.4) | copy-start | bytes 147460
  2.2 7.6 %copy-start.1 = (bf16[32,512]{1,0:T(8,128)(2,1)S(1)}, bf16[32,512]{1,0:T(8,128)(2,1)}, u32[]{:S(2)}) copy-start(bf16[32,512]{1,0:T(8,128)(2,1)} %param.5) | copy-start | bytes 98308
  2.2 41.7 %all-to-all-start = ((bf16[8,128,768]{2,1,0:T(8,128)(2,1)}), bf16[8,128,768]{2,1,0:T(8,128)(2,1)S(1)}, u32[]{:S(2)}, u32[]{:S(2)}) async-start(bf16[8,128,768]{2,1,0:T(8,128)(2,1)} %broadcast_in_dim.2), calls=%async_computation | async-start | bytes 3145728 | tf_op jit(solution)/shard_map/all_to_all | solution.py:26
  43.9 18.5 %collective-permute-start.2 = (bf16[256,1280]{1,0:T(8,128)(2,1)S(1)}, bf16[256,1280]{1,0:T(8,128)(2,1)S(1)}, u32[]{:S(2)}, u32[]{:S(2)}) collective-permute-start(bf16[256,1280]{1,0:T(8,128)(2,1)S(1)} %all_gather.3.refs_0_), channel_id=1, source_target_pairs={{0,496},{16,256},{32,272},{48,288},{64,304},{80,320},{96,336},{112... | collective-permute-start | bytes 1966088 | tf_op jit(solution)/shard_map/ppermute | solution.py:37
  47.3 15.1 %collective-permute-start.1 = (bf16[256,1280]{1,0:T(8,128)(2,1)S(1)}, bf16[256,1280]{1,0:T(8,128)(2,1)S(1)}, u32[]{:S(2)}, u32[]{:S(2)}) collective-permute-start(bf16[256,1280]{1,0:T(8,128)(2,1)S(1)} %all_gather.3.refs_0_), channel_id=1, source_target_pairs={{0,16},{16,32},{32,48},{48,64},{64,80},{80,96},{96,112},{112,128},... | collective-permute-start | bytes 1966088 | tf_op jit(solution)/shard_map/ppermute | solution.py:37
  49.3 13.3 %collective-permute-start = (bf16[256,1280]{1,0:T(8,128)(2,1)S(1)}, bf16[256,1280]{1,0:T(8,128)(2,1)S(1)}, u32[]{:S(2)}, u32[]{:S(2)}) collective-permute-start(bf16[256,1280]{1,0:T(8,128)(2,1)S(1)} %all_gather.3.refs_0_), channel_id=1, source_target_pairs={{0,257},{16,273},{32,289},{48,305},{64,321},{80,337},{96,353},{112... | collective-permute-start | bytes 1966088 | tf_op jit(solution)/shard_map/ppermute | solution.py:37
  54.9 9.2 %collective-permute-start.3 = (bf16[256,1280]{1,0:T(8,128)(2,1)S(1)}, bf16[256,1280]{1,0:T(8,128)(2,1)S(1)}, u32[]{:S(2)}, u32[]{:S(2)}) collective-permute-start(bf16[256,1280]{1,0:T(8,128)(2,1)S(1)} %all_gather.3.refs_0_), channel_id=1, source_target_pairs={{0,8},{8,0},{1,9},{9,1},{2,10},{10,2},{3,11},{11,3},{4,12},{12,4},... | collective-permute-start | bytes 1966088 | tf_op jit(solution)/shard_map/ppermute | solution.py:49
  64.2 10.5 %collective-permute-start.4 = (bf16[768,1280]{1,0:T(8,128)(2,1)S(1)}, bf16[768,1280]{1,0:T(8,128)(2,1)S(1)}, u32[]{:S(2)}, u32[]{:S(2)}) collective-permute-start(bf16[768,1280]{1,0:T(8,128)(2,1)S(1)} %constant_dynamic-update-slice_fusion.refs_0_), channel_id=1, source_target_pairs={{0,8},{8,0},{1,9},{9,1},{2,10},{10,2},{3,11},{11,3},{4,12},{12,4},... | collective-permute-start | bytes 5898248 | tf_op jit(solution)/shard_map/ppermute | solution.py:49
